TPU v7x, 128 devices: a whole 4x4x4 slice. The times are simulated.
128 devices in a mesh: ta: 16 (over y_hi, x, core), col: 8 (over y_lo, z).
Axes of the slice: x: 4, y: 4 (y_hi: 2, y_lo: 2; y = y_hi * 2 + y_lo), z: 4, core: 2. Of those that a mesh axis runs over, the one named last changes fastest.
Arguments:
- big_tokens: bfloat16 [8, 2048, 1024], P('col', 'ta'), may hold values from -6 to 6
- small_tokens: bfloat16 [32, 512, 1024], P('col', 'ta'), may hold values from -6 to 6
- big_actions: int32 [8, 8], P('col'), may hold values from 0 to 7
- small_actions: int32 [32, 8], P('col'), may hold values from 0 to 7
- big_order: int32 [8, 8], P('col'), may hold values from 0 to 7, each once within a row
- small_order: int32 [32, 8], P('col'), may hold values from 0 to 7, each once within a row
- small_live: int32 [32], P('col'), may hold values from 0 to 1, as said below
- action_table: bfloat16 [8, 1024], replicated, may hold values from -6 to 6
- norm1_gain: bfloat16 [1024], replicated, may hold values from 0.099609375 to 1.8984375
- norm1_bias: bfloat16 [1024], replicated, may hold values from -3 to 3
- spatial_qkv: bfloat16 [1024, 3072], replicated, may hold values from -0.1875 to 0.1875
- spatial_out: bfloat16 [1024, 1024], replicated, may hold values from -0.5 to 0.5
- spatial_out_bias: bfloat16 [1024], replicated, may hold values from -3 to 3
- norm2_gain: bfloat16 [1024], replicated, may hold values from 0.099609375 to 1.8984375
- norm2_bias: bfloat16 [1024], replicated, may hold values from -3 to 3
- temporal_qkv: bfloat16 [1024, 3072], replicated, may hold values from -0.1875 to 0.1875
- temporal_out: bfloat16 [1024, 1024], replicated, may hold values from -0.375 to 0.375
- temporal_out_bias: bfloat16 [1024], replicated, may hold values from -3 to 3
- norm3_gain: bfloat16 [1024], replicated, may hold values from 0.099609375 to 1.8984375
- norm3_bias: bfloat16 [1024], replicated, may hold values from -3 to 3
- ffn_in: bfloat16 [1024, 4096], replicated, may hold values from -0.1875 to 0.1875
- ffn_in_bias: bfloat16 [4096], replicated, may hold values from -3 to 3
- ffn_out: bfloat16 [4096, 1024], replicated, may hold values from -0.09375 to 0.09375
- ffn_out_bias: bfloat16 [1024], replicated, may hold values from -3 to 3
- big_cotangent: bfloat16 [8, 2048, 1024], P('col', 'ta'), may hold values from -6 to 6
- small_cotangent: bfloat16 [32, 512, 1024], P('col', 'ta'), may hold values from -6 to 6
Outputs:
- big_output: bfloat16 [8, 2048, 1024], P('col', 'ta')
- small_output: bfloat16 [32, 512, 1024], P('col', 'ta')
- big_input_grad: float32 [8, 2048, 1024], P('col', 'ta')
- small_input_grad: float32 [32, 512, 1024], P('col', 'ta')
- action_table_grad: float32 [8, 1024], replicated
- norm1_gain_grad: float32 [1024], replicated
- norm1_bias_grad: float32 [1024], replicated
- spatial_qkv_grad: float32 [1024, 3072], P('col')
- spatial_out_grad: float32 [1024, 1024], P('col')
- spatial_out_bias_grad: float32 [1024], replicated
- norm2_gain_grad: float32 [1024], replicated
- norm2_bias_grad: float32 [1024], replicated
- temporal_qkv_grad: float32 [1024, 3072], P('col')
- temporal_out_grad: float32 [1024, 1024], P('col')
- temporal_out_bias_grad: float32 [1024], replicated
- norm3_gain_grad: float32 [1024], replicated
- norm3_bias_grad: float32 [1024], replicated
- ffn_in_grad: float32 [1024, 4096], P('col')
- ffn_in_bias_grad: float32 [4096], replicated
- ffn_out_grad: float32 [4096, 1024], P('col')
- ffn_out_bias_grad: float32 [1024], replicated
Inputs may be any that keep to these rules, and one draw needn't show every extreme that they name: `small_live`: the small slots of one index of col hold their clips first; each index of col holds 0 to 4 clips, some index holds 4, and some other index holds fewer than 4.
All inputs are finite; a program needn't handle non-finite values.
Results may differ from a plain program's by a relative error of at most 0.024.
Values may be sent and summed in bfloat16 or wider, within the bound.
A program may use at most 384 MiB of HBM per device.

v0:
```python
import jax
import jax.numpy as jnp
from jax import lax
from jax.sharding import PartitionSpec as P

HEAD_DIM = 64


EPSILON = 1e-05
MASKED_SCORE = -1e30
SPATIAL_FORMS = ("bqhe", "bkhe", "bhqk")
TEMPORAL_FORMS = ("sfmhe", "sgmhe", "smhfg")


def from_partner(value, axis, apart):
    mask = 2**apart
    pairs = [(source, source ^ mask) for source in range(lax.axis_size(axis))]
    return lax.ppermute(value, axis, pairs)


def in_order(pieces, dim):
    shape = list(pieces.shape[1:])
    shape[dim] *= pieces.shape[0]
    return jnp.moveaxis(pieces, 0, dim).reshape(shape)


def one_gather(arrays, axis, dims):
    ravelled = jnp.concatenate([a.reshape(-1) for a in arrays])
    lines, at, finished = (lax.all_gather(ravelled, axis), 0, [])
    for a, dim in zip(arrays, dims):
        pieces = lines[:, at : at + a.size].reshape(-1, *a.shape)
        finished.append(in_order(pieces, dim))
        at += a.size
    return tuple(finished)


def normalize(rows, gain, shift):
    mean_row = jnp.mean(rows, axis=-1, keepdims=True)
    centered = rows - mean_row
    variance = jnp.mean(centered * centered, axis=-1, keepdims=True)
    return centered * lax.rsqrt(variance + EPSILON) * gain + shift


def norm_backward(rows, gain, shift, gradient):
    unused_value, pullback = jax.vjp(normalize, rows, gain, shift)
    return pullback(gradient)


def project(activation, weight):
    return jnp.einsum("...k,kn->...n", activation, weight, preferred_element_type=jnp.float32)


def project_back(gradient, weight):
    return jnp.einsum("...n,kn->...k", gradient, weight, preferred_element_type=jnp.float32)


def weight_grad(activation, gradient):
    flat_act = activation.reshape(-1, activation.shape[-1])
    flat_grad = gradient.reshape(-1, gradient.shape[-1])
    return lax.dot_general(
        flat_act, flat_grad, (((0,), (0,)), ((), ())), preferred_element_type=jnp.float32
    )


def column_sum(gradient):
    return jnp.sum(gradient.reshape(-1, gradient.shape[-1]), axis=0)


def score_rows(queries, key_rows, visible, layouts):
    query_form, key_form, score_form = layouts
    scale_factor = queries.shape[-1] ** (-0.5)
    scores = (
        jnp.einsum(
            query_form + "," + key_form + "->" + score_form,
            queries,
            key_rows,
            preferred_element_type=jnp.float32,
        )
        * scale_factor
    )
    return jnp.where(visible, scores, MASKED_SCORE)


def attend_forward(queries, key_rows, value_rows, visible, layouts):
    query_form, key_form, score_form = layouts
    scores = score_rows(queries, key_rows, visible, layouts)
    row_max = jnp.max(scores, axis=-1, keepdims=True)
    weights = jnp.exp(scores - row_max)
    row_total = jnp.sum(weights, axis=-1, keepdims=True)
    probability = (weights / row_total).astype(jnp.bfloat16)
    context = jnp.einsum(
        score_form + "," + key_form + "->" + query_form,
        probability,
        value_rows,
        preferred_element_type=jnp.float32,
    )
    return (context.astype(jnp.bfloat16), row_max + jnp.log(row_total))


def attend_backward(queries, key_rows, value_rows, visible, layouts, log_total, context_grad):
    query_form, key_form, score_form = layouts
    scale_factor = queries.shape[-1] ** (-0.5)
    probability = jnp.exp(score_rows(queries, key_rows, visible, layouts) - log_total)
    prob_grad = jnp.einsum(
        query_form + "," + key_form + "->" + score_form,
        context_grad,
        value_rows,
        preferred_element_type=jnp.float32,
    )
    row_delta = jnp.sum(probability * prob_grad, axis=-1, keepdims=True)
    score_grad = (probability * (prob_grad - row_delta)).astype(jnp.bfloat16)
    low_prob = probability.astype(jnp.bfloat16)
    query_grad = (
        jnp.einsum(
            score_form + "," + key_form + "->" + query_form,
            score_grad,
            key_rows,
            preferred_element_type=jnp.float32,
        )
        * scale_factor
    )
    key_grad = (
        jnp.einsum(
            score_form + "," + query_form + "->" + key_form,
            score_grad,
            queries,
            preferred_element_type=jnp.float32,
        )
        * scale_factor
    )
    value_grad = jnp.einsum(
        score_form + "," + query_form + "->" + key_form,
        low_prob,
        context_grad,
        preferred_element_type=jnp.float32,
    )
    return (query_grad, key_grad, value_grad)


def regroup(gradient, col_count, ta_count):
    return jnp.swapaxes(gradient.reshape(col_count, ta_count, -1), 0, 1).reshape(-1)


def body(
    big_tokens,
    small_tokens,
    big_actions,
    small_actions,
    big_order,
    small_order,
    small_live,
    action_table,
    norm1_gain,
    norm1_bias,
    spatial_qkv,
    spatial_out,
    spatial_out_bias,
    norm2_gain,
    norm2_bias,
    temporal_qkv,
    temporal_out,
    temporal_out_bias,
    norm3_gain,
    norm3_bias,
    ffn_in,
    ffn_in_bias,
    ffn_out,
    ffn_out_bias,
    big_cotangent,
    small_cotangent,
):
    model_width = big_tokens.shape[2]
    head_count = model_width // HEAD_DIM
    ta_count = lax.axis_size("ta")
    col_count = lax.axis_size("col")
    frame_count = big_actions.shape[1]
    frame_index = lax.axis_index("ta") // 2
    gain_one = norm1_gain.astype(jnp.float32)
    shift_one = norm1_bias.astype(jnp.float32)
    gain_two = norm2_gain.astype(jnp.float32)
    shift_two = norm2_bias.astype(jnp.float32)
    gain_three = norm3_gain.astype(jnp.float32)
    shift_three = norm3_bias.astype(jnp.float32)
    bias_spatial = spatial_out_bias.astype(jnp.float32)
    bias_temporal = temporal_out_bias.astype(jnp.float32)
    bias_inner = ffn_in_bias.astype(jnp.float32)
    bias_outer = ffn_out_bias.astype(jnp.float32)
    alive = small_live.astype(jnp.float32)[:, None, None]
    token_sets = (big_tokens, small_tokens)
    action_sets = (big_actions, small_actions)
    order_sets = (big_order, small_order)
    cotangent_sets = (
        big_cotangent.astype(jnp.float32),
        small_cotangent.astype(jnp.float32) * alive,
    )
    chosen = jnp.arange(frame_count)[None, :] == frame_index
    action_range = jnp.arange(action_table.shape[0])[None, :]
    picks, resid_zero, normed_one, packed_one = ([], [], [], [])
    for family in range(2):
        action_now = jnp.sum(jnp.where(chosen, action_sets[family], 0), axis=1)
        action_pick = (action_now[:, None] == action_range).astype(jnp.bfloat16)
        embedding = jnp.dot(action_pick, action_table, preferred_element_type=jnp.float32)
        rows_zero = token_sets[family].astype(jnp.float32) + embedding[:, None, :]
        normed = normalize(rows_zero, gain_one, shift_one).astype(jnp.bfloat16)
        picks.append(action_pick)
        resid_zero.append(rows_zero)
        normed_one.append(normed)
        packed_one.append(project(normed, spatial_qkv).astype(jnp.bfloat16))
    far_rows = from_partner(
        (packed_one[0][:, :, model_width:], packed_one[1][:, :, model_width:]), "ta", 0
    )
    spatial_saved, context_one, resid_one, sends = ([], [], [], [])
    for family in range(2):
        slot_count, row_count = (packed_one[family].shape[0], packed_one[family].shape[1])
        joined = jnp.concatenate([packed_one[family][:, :, model_width:], far_rows[family]], axis=1)
        queries = packed_one[family][:, :, :model_width].reshape(
            slot_count, row_count, head_count, HEAD_DIM
        )
        key_rows = joined[:, :, :model_width].reshape(
            slot_count, 2 * row_count, head_count, HEAD_DIM
        )
        value_rows = joined[:, :, model_width:].reshape(
            slot_count, 2 * row_count, head_count, HEAD_DIM
        )
        context, log_total = attend_forward(queries, key_rows, value_rows, True, SPATIAL_FORMS)
        context = context.reshape(slot_count, row_count, model_width)
        spatial_saved.append((queries, key_rows, value_rows, log_total))
        context_one.append(context)
        rows_one = resid_zero[family] + project(context, spatial_out) + bias_spatial
        resid_one.append(rows_one)
        normed = normalize(rows_one, gain_two, shift_two).astype(jnp.bfloat16)
        sends.append(normed.reshape(slot_count, ta_count, row_count // ta_count, model_width))
    moved = (
        lax.all_to_all(sends[0], "ta", split_axis=1, concat_axis=1, tiled=True),
        lax.all_to_all(sends[1], "ta", split_axis=1, concat_axis=1, tiled=True),
    )
    temporal_saved, arranged_two, returns = ([], [], [])
    for family in range(2):
        slot_count = moved[family].shape[0]
        arranged = moved[family].reshape(slot_count, frame_count, -1, model_width)
        shape_heads = (slot_count, frame_count, arranged.shape[2], head_count, HEAD_DIM)
        packed = project(arranged, temporal_qkv).astype(jnp.bfloat16)
        queries = packed[..., :model_width].reshape(shape_heads)
        key_rows = packed[..., model_width : 2 * model_width].reshape(shape_heads)
        value_rows = packed[..., 2 * model_width :].reshape(shape_heads)
        frame_order = order_sets[family]
        visible = (frame_order[:, None, :] <= frame_order[:, :, None])[:, None, None, :, :]
        context, log_total = attend_forward(queries, key_rows, value_rows, visible, TEMPORAL_FORMS)
        temporal_saved.append((queries, key_rows, value_rows, visible, log_total))
        arranged_two.append(arranged)
        returns.append(context.reshape(slot_count, ta_count, -1, model_width))
    back_rows = (
        lax.all_to_all(returns[0], "ta", split_axis=1, concat_axis=1, tiled=True),
        lax.all_to_all(returns[1], "ta", split_axis=1, concat_axis=1, tiled=True),
    )
    context_two, resid_two, normed_three, hidden_sets, activated_sets, results = (
        [],
        [],
        [],
        [],
        [],
        [],
    )
    for family in range(2):
        slot_count, row_count = (resid_one[family].shape[0], resid_one[family].shape[1])
        context = back_rows[family].reshape(slot_count, row_count, model_width)
        rows_two = resid_one[family] + project(context, temporal_out) + bias_temporal
        normed = normalize(rows_two, gain_three, shift_three).astype(jnp.bfloat16)
        hidden = project(normed, ffn_in) + bias_inner
        activated = jax.nn.gelu(hidden).astype(jnp.bfloat16)
        results.append(rows_two + project(activated, ffn_out) + bias_outer)
        context_two.append(context)
        resid_two.append(rows_two)
        normed_three.append(normed)
        hidden_sets.append(hidden)
        activated_sets.append(activated)
    outer_terms, inner_terms, outer_bias_terms, inner_bias_terms = ([], [], [], [])
    gain3_terms, shift3_terms, tbias_terms, tout_terms = ([], [], [], [])
    grad_two_sets, sends_back = ([], [])
    for family in range(2):
        grad_three = cotangent_sets[family]
        grad_low = grad_three.astype(jnp.bfloat16)
        outer_bias_terms.append(column_sum(grad_three))
        outer_terms.append(weight_grad(activated_sets[family], grad_low))
        act_grad = project_back(grad_low, ffn_out)
        unused_value, gelu_pull = jax.vjp(jax.nn.gelu, hidden_sets[family])
        hidden_grad = gelu_pull(act_grad)[0]
        inner_bias_terms.append(column_sum(hidden_grad))
        hidden_low = hidden_grad.astype(jnp.bfloat16)
        inner_terms.append(weight_grad(normed_three[family], hidden_low))
        rows_grad, gain_grad, shift_grad = norm_backward(
            resid_two[family], gain_three, shift_three, project_back(hidden_low, ffn_in)
        )
        gain3_terms.append(gain_grad)
        shift3_terms.append(shift_grad)
        grad_two = grad_three + rows_grad
        grad_two_sets.append(grad_two)
        tbias_terms.append(column_sum(grad_two))
        grad_two_low = grad_two.astype(jnp.bfloat16)
        tout_terms.append(weight_grad(context_two[family], grad_two_low))
        context_grad = project_back(grad_two_low, temporal_out).astype(jnp.bfloat16)
        slot_count, row_count = (grad_two.shape[0], grad_two.shape[1])
        sends_back.append(
            context_grad.reshape(slot_count, ta_count, row_count // ta_count, model_width)
        )
    context_moved = (
        lax.all_to_all(sends_back[0], "ta", split_axis=1, concat_axis=1, tiled=True),
        lax.all_to_all(sends_back[1], "ta", split_axis=1, concat_axis=1, tiled=True),
    )
    tqkv_terms, normed_back = ([], [])
    for family in range(2):
        queries, key_rows, value_rows, visible, log_total = temporal_saved[family]
        context_grad = context_moved[family].reshape(queries.shape)
        query_grad, key_grad, value_grad = attend_backward(
            queries, key_rows, value_rows, visible, TEMPORAL_FORMS, log_total, context_grad
        )
        flat_shape = queries.shape[:3] + (model_width,)
        packed_grad = jnp.concatenate(
            [
                query_grad.reshape(flat_shape),
                key_grad.reshape(flat_shape),
                value_grad.reshape(flat_shape),
            ],
            axis=-1,
        ).astype(jnp.bfloat16)
        tqkv_terms.append(weight_grad(arranged_two[family], packed_grad))
        normed_grad = project_back(packed_grad, temporal_qkv).astype(jnp.bfloat16)
        normed_back.append(normed_grad.reshape(queries.shape[0], ta_count, -1, model_width))
    normed_frames = (
        lax.all_to_all(normed_back[0], "ta", split_axis=1, concat_axis=1, tiled=True),
        lax.all_to_all(normed_back[1], "ta", split_axis=1, concat_axis=1, tiled=True),
    )
    gain2_terms, shift2_terms, sbias_terms, sout_terms = ([], [], [], [])
    far_sends, spatial_grads = ([], [])
    for family in range(2):
        slot_count, row_count = (resid_one[family].shape[0], resid_one[family].shape[1])
        normed_grad = (
            normed_frames[family].reshape(slot_count, row_count, model_width).astype(jnp.float32)
        )
        rows_grad, gain_grad, shift_grad = norm_backward(
            resid_one[family], gain_two, shift_two, normed_grad
        )
        gain2_terms.append(gain_grad)
        shift2_terms.append(shift_grad)
        grad_one = grad_two_sets[family] + rows_grad
        sbias_terms.append(column_sum(grad_one))
        grad_one_low = grad_one.astype(jnp.bfloat16)
        sout_terms.append(weight_grad(context_one[family], grad_one_low))
        queries, key_rows, value_rows, log_total = spatial_saved[family]
        context_grad = (
            project_back(grad_one_low, spatial_out).astype(jnp.bfloat16).reshape(queries.shape)
        )
        query_grad, key_grad, value_grad = attend_backward(
            queries, key_rows, value_rows, True, SPATIAL_FORMS, log_total, context_grad
        )
        near_shape = (slot_count, row_count, model_width)
        spatial_grads.append(
            (
                grad_one,
                query_grad.reshape(near_shape),
                key_grad[:, :row_count].reshape(near_shape),
                value_grad[:, :row_count].reshape(near_shape),
            )
        )
        far_sends.append(
            jnp.concatenate(
                [
                    key_grad[:, row_count:].reshape(near_shape),
                    value_grad[:, row_count:].reshape(near_shape),
                ],
                axis=-1,
            )
        )
    far_grads = (
        from_partner(far_sends[0].astype(jnp.bfloat16), "ta", 0).astype(jnp.float32),
        from_partner(far_sends[1].astype(jnp.bfloat16), "ta", 0).astype(jnp.float32),
    )
    sqkv_terms, gain1_terms, shift1_terms, table_terms, input_grads = ([], [], [], [], [])
    for family in range(2):
        grad_one, query_grad, key_near, value_near = spatial_grads[family]
        packed_grad = jnp.concatenate(
            [
                query_grad,
                key_near + far_grads[family][..., :model_width],
                value_near + far_grads[family][..., model_width:],
            ],
            axis=-1,
        ).astype(jnp.bfloat16)
        sqkv_terms.append(weight_grad(normed_one[family], packed_grad))
        rows_grad, gain_grad, shift_grad = norm_backward(
            resid_zero[family], gain_one, shift_one, project_back(packed_grad, spatial_qkv)
        )
        gain1_terms.append(gain_grad)
        shift1_terms.append(shift_grad)
        grad_zero = grad_one + rows_grad
        input_grads.append(grad_zero)
        table_terms.append(
            lax.dot_general(
                picks[family].astype(jnp.float32),
                jnp.sum(grad_zero, axis=1),
                (((0,), (0,)), ((), ())),
                preferred_element_type=jnp.float32,
            )
        )
    small_sums = lax.psum(
        (
            table_terms[0] + table_terms[1],
            gain1_terms[0] + gain1_terms[1],
            shift1_terms[0] + shift1_terms[1],
            sbias_terms[0] + sbias_terms[1],
            gain2_terms[0] + gain2_terms[1],
            shift2_terms[0] + shift2_terms[1],
            tbias_terms[0] + tbias_terms[1],
            gain3_terms[0] + gain3_terms[1],
            shift3_terms[0] + shift3_terms[1],
            inner_bias_terms[0] + inner_bias_terms[1],
            outer_bias_terms[0] + outer_bias_terms[1],
        ),
        ("ta", "col"),
    )
    grad_sqkv = sqkv_terms[0] + sqkv_terms[1]
    grad_sout = sout_terms[0] + sout_terms[1]
    grad_tqkv = tqkv_terms[0] + tqkv_terms[1]
    grad_tout = tout_terms[0] + tout_terms[1]
    grad_inner = inner_terms[0] + inner_terms[1]
    grad_outer = outer_terms[0] + outer_terms[1]
    pieces = (
        lax.psum_scatter(
            regroup(grad_sqkv, col_count, ta_count), ("ta", "col"), scatter_dimension=0, tiled=True
        ),
        lax.psum_scatter(
            regroup(grad_sout, col_count, ta_count), ("ta", "col"), scatter_dimension=0, tiled=True
        ),
        lax.psum_scatter(
            regroup(grad_tqkv, col_count, ta_count), ("ta", "col"), scatter_dimension=0, tiled=True
        ),
        lax.psum_scatter(
            regroup(grad_tout, col_count, ta_count), ("ta", "col"), scatter_dimension=0, tiled=True
        ),
        lax.psum_scatter(
            regroup(grad_inner, col_count, ta_count), ("ta", "col"), scatter_dimension=0, tiled=True
        ),
        lax.psum_scatter(
            regroup(grad_outer, col_count, ta_count), ("ta", "col"), scatter_dimension=0, tiled=True
        ),
    )
    whole = tuple(
        (
            part.astype(jnp.float32)
            for part in one_gather(
                (
                    pieces[0].astype(jnp.bfloat16),
                    pieces[1].astype(jnp.bfloat16),
                    pieces[2].astype(jnp.bfloat16),
                    pieces[3].astype(jnp.bfloat16),
                    pieces[4].astype(jnp.bfloat16),
                    pieces[5].astype(jnp.bfloat16),
                ),
                "ta",
                (0, 0, 0, 0, 0, 0),
            )
        )
    )
    full_shapes = (
        grad_sqkv.shape,
        grad_sout.shape,
        grad_tqkv.shape,
        grad_tout.shape,
        grad_inner.shape,
        grad_outer.shape,
    )
    totals = tuple(
        (
            whole[index_pos].reshape(
                full_shapes[index_pos][0] // col_count, full_shapes[index_pos][1]
            )
            for index_pos in range(6)
        )
    )
    return (
        results[0].astype(jnp.bfloat16),
        (results[1] * alive).astype(jnp.bfloat16),
        input_grads[0],
        input_grads[1],
        small_sums[0],
        small_sums[1],
        small_sums[2],
        totals[0],
        totals[1],
        small_sums[3],
        small_sums[4],
        small_sums[5],
        totals[2],
        totals[3],
        small_sums[6],
        small_sums[7],
        small_sums[8],
        totals[4],
        small_sums[9],
        totals[5],
        small_sums[10],
    )


def solution(mesh):
    return jax.shard_map(
        body,
        mesh=mesh,
        in_specs=(
            P("col", "ta", None),
            P("col", "ta", None),
            P("col", None),
            P("col", None),
            P("col", None),
            P("col", None),
            P("col"),
            P(),
            P(),
            P(),
            P(),
            P(),
            P(),
            P(),
            P(),
            P(),
            P(),
            P(),
            P(),
            P(),
            P(),
            P(),
            P(),
            P(),
            P("col", "ta", None),
            P("col", "ta", None),
        ),
        out_specs=(
            P("col", "ta", None),
            P("col", "ta", None),
            P("col", "ta", None),
            P("col", "ta", None),
            P(),
            P(),
            P(),
            P("col", None),
            P("col", None),
            P(),
            P(),
            P(),
            P("col", None),
            P("col", None),
            P(),
            P(),
            P(),
            P("col", None),
            P(),
            P("col", None),
            P(),
        ),
        check_vma=False,
    )
```

profile of v0, /device:TPU:1, one launch (start us, length us, event | category | flops | bytes accessed | tf_op | source)
XLA Modules:
  0.0 979.6 jit_solution(8698644568714760203)
XLA Ops:
  14.5 4.1 fusion.32
  37.0 8.0 all-to-all-start
  45.0 2.2 fusion.167
  47.3 2.5 reshape.1127
  49.8 2.5 reshape.1129
  58.0 2.2 fusion.304
  66.8 7.6 all-to-all-start.2
  74.4 3.9 fusion.33
  85.8 3.9 fusion.29
  92.7 2.1 reshape.1134
  104.8 7.2 all-to-all-start.3
  123.3 8.0 all-to-all-start.1
  134.9 4.9 fusion.20
  139.9 8.2 fusion.247
  148.1 4.2 fusion.308
  152.3 8.3 fusion.179
  160.6 3.7 fusion.290
  166.8 4.9 convolution_add_fusion.1
  171.7 7.8 fusion.307
  179.6 3.0 fusion.173
  186.2 7.2 all-to-all-start.4
  199.6 14.5 %bitcast_add_fusion.1 = f32[1024,4096]{1,0:T(8,128)} fusion(f32[1024,4096,1]{1,0,2:T(8,128)} %fusion.179, bf16[128,4096]{1,0:T(8,128)(2,1)} %copy-done.48, f32[1,128,1024]{2,1,0:T(8,128)S(1)} %get-tuple-element.98, f32[1024]{0:T(1024)S(1)} %convert_element_type.359, f32[1024]{0:T(1024)S(1)} %convert_element_type.358, f32[128]{0:T(128)S(1)} %fusion.272, ...), kind=kOutput, calls=%fused_computation.1 | convolution fusion | flops 1078591488 | bytes 35136512 | tf_op jit(solution)/shard_map/dot_general | solution.py:60
  214.1 14.0 %bitcast_add_fusion = f32[4096,1024]{1,0:T(8,128)} fusion(f32[4096,1024,1]{1,0,2:T(8,128)} %fusion.247, bf16[1,128,1024]{2,1,0:T(8,128)(2,1)S(1)} %copy-done.49, f32[128,4096]{1,0:T(8,128)S(1)} %copy-done.18), kind=kOutput, calls=%fused_computation | convolution fusion | flops 1082654720 | bytes 35913728 | tf_op jit(solution)/shard_map/dot_general | solution.py:60
  229.9 2.8 convolution_add_fusion.2
  232.7 5.0 reshape.1167
  237.7 4.6 copy.459
  242.3 2.7 copy.361
  245.0 18.2 %reshape.1169 = f32[8,16,32768]{2,1,0:T(8,128)} reshape(f32[1024,4096]{1,0:T(8,128)} %bitcast_add_fusion.1) | data formatting | bytes 33554432 | tf_op jit(solution)/shard_map/reshape | solution.py:141
  263.2 15.6 %copy.456 = f32[8,16,32768]{2,0,1:T(8,128)S(1)} copy(f32[8,16,32768]{2,1,0:T(8,128)} %reshape.1169) | data formatting | bytes 33554432 | tf_op jit(solution)/shard_map/reshape | solution.py:141
  278.8 6.8 copy.362
  285.6 18.2 %reshape.1171 = f32[8,16,32768]{2,1,0:T(8,128)} reshape(f32[4096,1024]{1,0:T(8,128)} %bitcast_add_fusion) | data formatting | bytes 33554432 | tf_op jit(solution)/shard_map/reshape | solution.py:141
  303.8 15.2 %copy.455 = f32[8,16,32768]{2,0,1:T(8,128)S(1)} copy(f32[8,16,32768]{2,1,0:T(8,128)} %reshape.1171) | data formatting | bytes 33554432 | tf_op jit(solution)/shard_map/reshape | solution.py:141
  319.1 6.8 copy.363
  326.0 7.7 all-to-all-start.6
  356.5 5.7 fusion.119
  362.2 6.4 all-to-all-start.5
  373.3 5.0 fusion.106
  378.3 2.8 fusion.147
  381.2 6.4 convolution_add_fusion
  388.4 12.4 %reshape.1164 = f32[8,16,24576]{2,1,0:T(8,128)} reshape(f32[1024,3072]{1,0:T(8,128)} %convolution_add_fusion) | data formatting | bytes 25165824 | tf_op jit(solution)/shard_map/reshape | solution.py:141
  400.8 16.4 %copy.457 = f32[8,16,24576]{2,0,1:T(8,128)} copy(f32[8,16,24576]{2,1,0:T(8,128)} %reshape.1164) | data formatting | bytes 25165824 | tf_op jit(solution)/shard_map/reshape | solution.py:141
  417.2 11.4 %copy.360 = f32[16,192,8,128]{3,1,2,0:T(8,128)} copy(f32[16,192,8,128]{3,2,1,0:T(8,128)} %bitcast.442) | data formatting | bytes 25165824
  428.6 7.4 all-to-all-start.7
  437.7 2.6 convolution_convert_fusion.6
  462.2 2.6 fusion.228
  474.4 4.9 convolution_add_fusion.3
  479.3 5.2 reshape.1162
  484.4 4.8 copy.460
  489.3 2.8 copy.359
  495.4 2.4 fusion.175
  502.7 2.4 fusion.291
  506.6 6.9 bitcast_add_fusion.2
  513.4 12.0 %reshape.1159 = f32[8,16,24576]{2,1,0:T(8,128)} reshape(f32[1024,3072]{1,0:T(8,128)} %bitcast_add_fusion.2) | data formatting | bytes 25165824 | tf_op jit(solution)/shard_map/reshape | solution.py:141
  525.4 16.4 %copy.458 = f32[8,16,24576]{2,0,1:T(8,128)} copy(f32[8,16,24576]{2,1,0:T(8,128)} %reshape.1159) | data formatting | bytes 25165824 | tf_op jit(solution)/shard_map/reshape | solution.py:141
  541.8 11.3 %copy.358 = f32[16,192,8,128]{3,1,2,0:T(8,128)} copy(f32[16,192,8,128]{3,2,1,0:T(8,128)} %bitcast.443) | data formatting | bytes 25165824
  553.3 336.8 %all-reduce.8 = (f32[8,1024]{1,0:T(8,128)}, f32[1024]{0:T(1024)}, f32[1024]{0:T(1024)}, bf16[3145728]{0:T(1024)(128)(2,1)}, bf16[1048576]{0:T(1024)(128)(2,1)}, ...) all-reduce(f32[8,1024]{1,0:T(8,128)S(1)} %convolution_add_fusion.4,, ...), channel_id=1, replica_groups=mesh['ta'=16,'col'=8] {'ta','col'}, use_global_device_ids=true, to_apply=%region_40.41 | all-reduce | flops 16798720 | bytes 100835328 | tf_op jit(solution)/shard_map/psum | solution.py:405
  895.7 6.4 fusion.105
  902.1 5.9 fusion.110
  908.0 42.9 %all-gather.3.cloned.1.call-done = bf16[2097152]{0:T(1024)(128)(2,1)} async-done(((bf16[131072]{0:T(1024)(128)(2,1)}), bf16[2097152]{0:T(1024)(128)(2,1)}) %all-gather.3.cloned.1.call-update) | async-done | bytes 4194320 | tf_op jit(solution)/shard_map/all_gather | solution.py:29
  950.9 4.7 reshape.1184
  955.6 3.4 slice_convert_fusion.4
  960.7 2.8 reshape.1175
  964.4 2.8 reshape.1177
  969.6 2.9 reshape.1180
  (581 shorter events, 167.4 us)
Async XLA Ops:
  7.2 126.0 %copy-start = (bf16[1024,1024]{1,0:T(8,128)(2,1)S(1)}, bf16[1024,1024]{1,0:T(8,128)(2,1)}, u32[]{:S(2)}) copy-start(bf16[1024,1024]{1,0:T(8,128)(2,1)} %param.42) | copy-start | bytes 6291460
  8.0 13.9 %copy-start.81 = (f32[1024]{0:T(1024)}, f32[1024]{0:T(1024)S(1)}, u32[]{:S(2)}) copy-start(f32[1024]{0:T(1024)S(1)} %convert_element_type.339) | copy-start | bytes 12292
  8.7 13.2 %copy-start.56 = (f32[1024]{0:T(1024)}, f32[1024]{0:T(1024)S(1)}, u32[]{:S(2)}) copy-start(f32[1024]{0:T(1024)S(1)} %convert_element_type.338) | copy-start | bytes 12292
  11.5 23.4 %copy-start.94 = (f32[1,1024]{1,0:T(1,128)}, f32[1,1024]{1,0:T(1,128)S(1)}, u32[]{:S(2)}) copy-start(f32[1,1024]{1,0:T(1,128)S(1)} %fusion.259) | copy-start | bytes 12292
  12.6 9.3 slice-start.4
  14.4 6.6 copy-start.126
  14.4 7.1 copy-start.24
  14.5 7.5 slice-start.5
  19.4 8.6 collective-permute-start
  21.5 36.5 %copy-start.92 = (f32[4,1024]{1,0:T(4,128)}, f32[4,1024]{1,0:T(4,128)S(1)}, u32[]{:S(2)}) copy-start(f32[4,1024]{1,0:T(4,128)S(1)} %fusion.258) | copy-start | bytes 49156
  24.1 20.9 %collective-permute-start.1 = (bf16[4,32,2048]{2,1,0:T(8,128)(2,1)}, bf16[4,32,2048]{2,1,0:T(8,128)(2,1)}, u32[]{:S(2)}, u32[]{:S(2)}) collective-permute-start(bf16[4,32,2048]{2,1,0:T(8,128)(2,1)} %slice.142), channel_id=1, source_target_pairs={{0,8},{8,0},{16,24},{24,16},{32,40},{40,32},{48,56},{56,48},{64,72... | collective-permute-start | bytes 1572872 | tf_op jit(solution)/shard_map/ppermute | solution.py:18
  24.4 8.0 copy-start.54
  24.4 36.1 %copy-start.100 = (f32[1024]{0:T(1024)}, f32[1024]{0:T(1024)S(1)}, u32[]{:S(2)}) copy-start(f32[1024]{0:T(1024)S(1)} %convert_element_type.348) | copy-start | bytes 12292
  35.9 129.2 %copy-start.10 = (f32[1,128,1024]{2,1,0:T(8,128)}, f32[1,128,1024]{2,1,0:T(8,128)S(1)}, u32[]{:S(2)}) copy-start(f32[1,128,1024]{2,1,0:T(8,128)S(1)} %get-tuple-element.94) | copy-start | bytes 1572868
  35.9 13.9 %copy-start.127 = (f32[128]{0:T(128)}, f32[128]{0:T(128)S(1)}, u32[]{:S(2)}) copy-start(f32[128]{0:T(128)S(1)} %broadcast_multiply_fusion.4) | copy-start | bytes 1540
  36.1 13.6 %copy-start.147 = (f32[128]{0:T(128)}, f32[128]{0:T(128)S(1)}, u32[]{:S(2)}) copy-start(f32[128]{0:T(128)S(1)} %multiply_reduce_fusion.15) | copy-start | bytes 1540
  36.2 13.6 %copy-start.131 = (f32[128]{0:T(128)}, f32[128]{0:T(128)S(1)}, u32[]{:S(2)}) copy-start(f32[128]{0:T(128)S(1)} %fusion.271) | copy-start | bytes 1540
  37.0 29.8 %all-to-all-start = ((bf16[1,16,8,1024]{3,2,0,1:T(8,128)(2,1)}), bf16[1,16,8,1024]{3,2,0,1:T(8,128)(2,1)}, u32[]{:S(2)}, u32[]{:S(2)}) async-start(bf16[1,16,8,1024]{3,2,0,1:T(8,128)(2,1)} %fusion.225), calls=%async_computation | async-start | bytes 524288 | tf_op jit(solution)/shard_map/all_to_all | solution.py:234
  60.3 72.9 %copy-start.12 = (f32[4,32,1024]{2,1,0:T(8,128)}, f32[4,32,1024]{2,1,0:T(8,128)S(1)}, u32[]{:S(2)}) copy-start(f32[4,32,1024]{2,1,0:T(8,128)S(1)} %get-tuple-element.102) | copy-start | bytes 1572868
  60.3 18.0 %copy-start.112 = (f32[4,32]{1,0:T(4,128)}, f32[4,32]{1,0:T(4,128)S(1)}, u32[]{:S(2)}) copy-start(f32[4,32]{1,0:T(4,128)S(1)} %broadcast_multiply_fusion.1) | copy-start | bytes 1540
  60.5 17.8 %copy-start.122 = (f32[4,32]{1,0:T(4,128)}, f32[4,32]{1,0:T(4,128)S(1)}, u32[]{:S(2)}) copy-start(f32[4,32]{1,0:T(4,128)S(1)} %multiply_reduce_fusion.12) | copy-start | bytes 1540
  60.5 17.8 %copy-start.114 = (f32[4,32]{1,0:T(4,128)}, f32[4,32]{1,0:T(4,128)S(1)}, u32[]{:S(2)}) copy-start(f32[4,32]{1,0:T(4,128)S(1)} %fusion.262) | copy-start | bytes 1540
  66.8 18.9 %all-to-all-start.2 = ((bf16[4,16,2,1024]{3,2,0,1:T(2,128)(2,1)}), bf16[4,16,2,1024]{3,2,0,1:T(2,128)(2,1)S(1)}, u32[]{:S(2)}, u32[]{:S(2)}) async-start(bf16[4,16,2,1024]{3,2,0,1:T(2,128)(2,1)} %copy.292), calls=%async_computation.2 | async-start | bytes 524288 | tf_op jit(solution)/shard_map/all_to_all | solution.py:235
  99.9 12.1 %copy-start.142 = (pred[8,8]{0,1:T(8,128)(4,1)S(1)}, pred[8,8]{0,1:T(8,128)(4,1)}, u32[]{:S(2)}) copy-start(pred[8,8]{0,1:T(8,128)(4,1)} %broadcast_compare_fusion.1) | copy-start | bytes 196
  104.8 18.5 %all-to-all-start.3 = ((bf16[4,16,2,1024]{3,2,0,1:T(2,128)(2,1)}), bf16[4,16,2,1024]{3,2,0,1:T(2,128)(2,1)}, u32[]{:S(2)}, u32[]{:S(2)}) async-start(bf16[4,16,2,1024]{3,2,0,1:T(2,128)(2,1)} %copy.300), calls=%async_computation.3 | async-start | bytes 524288 | tf_op jit(solution)/shard_map/all_to_all | solution.py:254
  123.3 41.8 %all-to-all-start.1 = ((bf16[1,16,8,1024]{3,2,0,1:T(8,128)(2,1)}), bf16[1,16,8,1024]{3,2,0,1:T(8,128)(2,1)}, u32[]{:S(2)}, u32[]{:S(2)}) async-start(bf16[1,16,8,1024]{3,2,0,1:T(8,128)(2,1)} %bitcast.467), calls=%async_computation.1 | async-start | bytes 524288 | tf_op jit(solution)/shard_map/all_to_all | solution.py:253
  134.7 25.9 %copy-start.14 = (f32[4,32,1024]{2,1,0:T(8,128)}, f32[4,32,1024]{2,1,0:T(8,128)S(1)}, u32[]{:S(2)}) copy-start(f32[4,32,1024]{2,1,0:T(8,128)S(1)} %get-tuple-element.106) | copy-start | bytes 1572868
  134.9 13.1 %slice-start.12 = ((s8[8388608]{0:T(1024)(128)(4,1)}), s8[4194304]{0:T(1024)(128)(4,1)S(1)}, s32[]{:S(2)}) async-start(s8[8388608]{0:T(1024)(128)(4,1)} %bitcast.482), calls=%async_computation.21 | async-start | bytes 8388608
  139.9 8.2 copy-start.58
  139.9 8.2 slice-start.13
  148.1 12.5 %slice-start = ((s8[8388608]{0:T(1024)(128)(4,1)}), s8[4194304]{0:T(1024)(128)(4,1)S(1)}, s32[]{:S(2)}) async-start(s8[8388608]{0:T(1024)(128)(4,1)} %bitcast.428), calls=%async_computation.9 | async-start | bytes 8388608
  152.3 8.3 slice-start.1
  166.6 33.0 %copy-start.6 = (f32[1,128,1024]{2,1,0:T(8,128)}, f32[1,128,1024]{2,1,0:T(8,128)S(1)}, u32[]{:S(2)}) copy-start(f32[1,128,1024]{2,1,0:T(8,128)S(1)} %get-tuple-element.98) | copy-start | bytes 1572868
  166.8 12.8 %slice-start.2 = ((s8[8388608]{0:T(1024)(128)(4,1)}), s8[4194304]{0:T(1024)(128)(4,1)S(1)}, s32[]{:S(2)}) async-start(s8[8388608]{0:T(1024)(128)(4,1)} %bitcast.430), calls=%async_computation.11 | async-start | bytes 8388608
  171.7 7.9 copy-start.17
  171.7 7.9 slice-start.3
  183.7 9.8 %copy-start.15 = (f32[4,32,1024]{2,1,0:T(8,128)S(1)}, f32[4,32,1024]{2,1,0:T(8,128)}, u32[]{:S(2)}) copy-start(f32[4,32,1024]{2,1,0:T(8,128)} %copy-done.14) | copy-start | bytes 1572868
  186.2 139.7 %all-to-all-start.4 = ((bf16[1,16,8,1024]{3,2,0,1:T(8,128)(2,1)}), bf16[1,16,8,1024]{3,2,0,1:T(8,128)(2,1)}, u32[]{:S(2)}, u32[]{:S(2)}) async-start(bf16[1,16,8,1024]{3,2,0,1:T(8,128)(2,1)} %fusion.122), calls=%async_computation.4 | async-start | bytes 524288 | tf_op jit(solution)/shard_map/all_to_all | solution.py:307
  199.6 14.5 %copy-start.18 = (f32[128,4096]{1,0:T(8,128)S(1)}, f32[128,4096]{1,0:T(8,128)}, u32[]{:S(2)}) copy-start(f32[128,4096]{1,0:T(8,128)} %copy-done.17) | copy-start | bytes 6291460
  214.1 14.0 %copy-start.34 = (f32[1,128,1024]{2,1,0:T(8,128)S(1)}, f32[1,128,1024]{2,1,0:T(8,128)}, u32[]{:S(2)}) copy-start(f32[1,128,1024]{2,1,0:T(8,128)} %copy-done.33) | copy-start | bytes 1572868
  319.1 6.8 copy-start.38
  319.1 15.9 %copy-start.79 = (f32[16,16,8]{2,1,0:T(8,128)S(1)}, f32[16,16,8]{2,1,0:T(8,128)}, u32[]{:S(2)}) copy-start(f32[16,16,8]{2,1,0:T(8,128)} %log_add_fusion.1) | copy-start | bytes 24580
  325.9 9.2 copy-start.23
  325.9 9.2 copy-start.77
  326.0 16.3 %all-to-all-start.6 = ((bf16[4,16,2,1024]{3,2,0,1:T(2,128)(2,1)}), bf16[4,16,2,1024]{3,2,0,1:T(2,128)(2,1)}, u32[]{:S(2)}, u32[]{:S(2)}) async-start(bf16[4,16,2,1024]{3,2,0,1:T(2,128)(2,1)} %copy.314), calls=%async_computation.6 | async-start | bytes 524288 | tf_op jit(solution)/shard_map/all_to_all | solution.py:308
  356.5 13.2 %copy-start.73 = (bf16[4,8,4,16,64]{4,3,1,2,0:T(8,128)(2,1)S(1)}, bf16[4,8,4,16,64]{4,3,1,2,0:T(8,128)(2,1)}, u32[]{:S(2)}) copy-start(bf16[4,8,4,16,64]{4,3,1,2,0:T(8,128)(2,1)} %copy.322) | copy-start | bytes 786436
  362.2 66.4 %all-to-all-start.5 = ((bf16[1,16,8,1024]{3,2,0,1:T(8,128)(2,1)}), bf16[1,16,8,1024]{3,2,0,1:T(8,128)(2,1)S(1)}, u32[]{:S(2)}, u32[]{:S(2)}) async-start(bf16[1,16,8,1024]{3,2,0,1:T(8,128)(2,1)} %bitcast.480), calls=%async_computation.5 | async-start | bytes 524288 | tf_op jit(solution)/shard_map/all_to_all | solution.py:330
  417.2 18.8 %copy-start.11 = (f32[1,128,1024]{2,1,0:T(8,128)S(1)}, f32[1,128,1024]{2,1,0:T(8,128)}, u32[]{:S(2)}) copy-start(f32[1,128,1024]{2,1,0:T(8,128)} %copy-done.10) | copy-start | bytes 1572868
  417.2 18.8 %copy-start.101 = (f32[1024]{0:T(1024)S(1)}, f32[1024]{0:T(1024)}, u32[]{:S(2)}) copy-start(f32[1024]{0:T(1024)} %copy-done.100) | copy-start | bytes 12292
  417.2 18.8 %copy-start.128 = (f32[128]{0:T(128)S(1)}, f32[128]{0:T(128)}, u32[]{:S(2)}) copy-start(f32[128]{0:T(128)} %copy-done.127) | copy-start | bytes 1540
  417.2 19.0 %copy-start.148 = (f32[128]{0:T(128)S(1)}, f32[128]{0:T(128)}, u32[]{:S(2)}) copy-start(f32[128]{0:T(128)} %copy-done.147) | copy-start | bytes 1540
  417.2 19.0 %copy-start.132 = (f32[128]{0:T(128)S(1)}, f32[128]{0:T(128)}, u32[]{:S(2)}) copy-start(f32[128]{0:T(128)} %copy-done.131) | copy-start | bytes 1540
  428.6 8.0 copy-start.50
  428.6 18.7 %all-to-all-start.7 = ((bf16[4,16,2,1024]{3,0,2,1:T(4,128)(2,1)}), bf16[4,16,2,1024]{3,0,2,1:T(4,128)(2,1)}, u32[]{:S(2)}, u32[]{:S(2)}) async-start(bf16[4,16,2,1024]{3,0,2,1:T(4,128)(2,1)} %bitcast.72), calls=%async_computation.7 | async-start | bytes 524288 | tf_op jit(solution)/shard_map/all_to_all | solution.py:331
  435.9 514.9 %all-gather.3.cloned.1.call-start = ((), (), s32[]{:S(2)}) async-start(), calls=%async_computation.8 | async-start | bytes 4456448 | tf_op jit(solution)/shard_map/all_gather | solution.py:29
  465.7 28.3 %collective-permute-start.2 = (bf16[1,128,2048]{1,2,0:T(8,128)(2,1)}, bf16[1,128,2048]{1,2,0:T(8,128)(2,1)}, u32[]{:S(2)}, u32[]{:S(2)}) collective-permute-start(bf16[1,128,2048]{1,2,0:T(8,128)(2,1)} %pad_maximum_fusion.4), channel_id=1, source_target_pairs={{0,8},{8,0},{16,24},{24,16},{32,40},{40,32},{48,56},{56,48},{64,72... | collective-permute-start | bytes 1572872 | tf_op jit(solution)/shard_map/ppermute | solution.py:18
  470.7 30.6 %collective-permute-start.3 = (bf16[4,32,2048]{2,1,0:T(8,128)(2,1)}, bf16[4,32,2048]{2,1,0:T(8,128)(2,1)}, u32[]{:S(2)}, u32[]{:S(2)}) collective-permute-start(bf16[4,32,2048]{2,1,0:T(8,128)(2,1)} %pad_maximum_fusion.5), channel_id=1, source_target_pairs={{0,8},{8,0},{16,24},{24,16},{32,40},{40,32},{48,56},{56,48},{64,72... | collective-permute-start | bytes 1572872 | tf_op jit(solution)/shard_map/ppermute | solution.py:18
  484.4 10.9 %slice-start.6 = ((s8[6291456]{0:T(1024)(128)(4,1)}), s8[4194304]{0:T(1024)(128)(4,1)S(1)}, s32[]{:S(2)}) async-start(s8[6291456]{0:T(1024)(128)(4,1)} %bitcast.438), calls=%async_computation.15 | async-start | bytes 8388608
  541.8 11.3 %copy-start.146 = (s32[4]{0:T(128)S(1)}, s32[4]{0:T(128)}, u32[]{:S(2)}) copy-start(s32[4]{0:T(128)} %copy-done.145) | copy-start | bytes 52
  541.8 11.3 %copy-start.152 = (f32[8]{0:T(128)S(1)}, f32[8]{0:T(128)}, u32[]{:S(2)}) copy-start(f32[8]{0:T(128)} %compare_convert_fusion) | copy-start | bytes 100
  553.3 342.3 %copy-start.139 = (bf16[1024]{0:T(1024)(128)(2,1)S(1)}, bf16[1024]{0:T(1024)(128)(2,1)}, u32[]{:S(2)}) copy-start(bf16[1024]{0:T(1024)(128)(2,1)} %param.49) | copy-start | bytes 6148
  553.3 342.3 %copy-start.7 = (f32[1,128,1024]{2,1,0:T(8,128)S(1)}, f32[1,128,1024]{2,1,0:T(8,128)}, u32[]{:S(2)}) copy-start(f32[1,128,1024]{2,1,0:T(8,128)} %copy-done.6) | copy-start | bytes 1572868
  895.6 6.5 copy-start.16
  895.7 6.4 copy-start.59
  (116 other events, 297.0 us)
Sparse Core Ops, SparseCore 0:
  895.7 55.0 all-gather.2
where the time goes:
time: 989 us; the launch traced here: 980 us
  blocking collectives  337 us (34%)
  local copies, waits for them, and re-layouts  294 us (30%)
  matrix products  183 us (19%)
  starting transfers between devices  61.4 us (6%)
  waiting for transfers between devices  44.2 us (4%)
  other arithmetic  42.7 us (4%)
  between operations  17 us (2%)
    psum x1, blocking collectives, body(): lax.psum((table_terms[0] + table_terms[1], gain1_terms[0] + gain1_terms[1...  337 us
    reshape x12, local copies, waits for them, and re-layouts, regroup(): gradient.reshape(col_count, ta_count, -1)  144 us
    dot_general x12, matrix products, weight_grad(): lax.dot_general(flat_act, flat_grad, (((0,), (0,)), ((), ())), preferred_...  75.1 us
    unnamed x341, local copies, waits for them, and re-layouts  56.5 us
    all_gather x1, waiting for transfers between devices, one_gather(): lines, at, finished = (lax.all_gather(ravelled, axis), 0, [])  42.9 us
    dot_general x12, matrix products, project_back(): jnp.einsum('...n,kn->...k', gradient, weight, preferred_element_type=jnp....  40.9 us
    dot_general x12, matrix products, project(): jnp.einsum('...k,kn->...n', activation, weight, preferred_element_type=jn...  40.8 us
  transfers between devices with their start and end apart: 13, of which 2 were waited for; matrix products, arithmetic and copies ran while one was open for 35% of the time, Pallas kernels for 0%

commit v1 on v0

v1 whole, which is shorter than its diff:
```python
import functools

import jax
import jax.numpy as jnp
from jax import lax
from jax.experimental import pallas as pl
from jax.experimental.pallas import tpu as pltpu
from jax.sharding import PartitionSpec as P

HEAD_DIM = 64
EPSILON = 1e-05
MASKED_SCORE = -1e30
MESH = pl.DeviceIdType.MESH
ANY = pl.BlockSpec(memory_space=pl.ANY)
LANES = 128
SPATIAL_FORMS = ("bqhe", "bkhe", "bhqk")

ORDERS = (("x", "y", "z"), ("y", "z", "x"), ("z", "x", "y"))
MATRICES = (
    ("ffn_out", (1, 1, 2)),
    ("ffn_in", (6, 6, 4)),
    ("temporal_out", (1, 2, 1)),
    ("temporal_qkv", (4, 4, 4)),
    ("spatial_out", (2, 1, 1)),
    ("spatial_qkv", (4, 4, 4)),
)


class Place:
    def __init__(self):
        ta, col = lax.axis_index("ta"), lax.axis_index("col")
        self.ta, self.col = ta, col
        self.y_hi, self.x, self.core = ta // 8, (ta // 2) % 4, ta % 2
        self.y_lo, self.z = col // 4, col % 4
        self.y = self.y_hi * 2 + self.y_lo

    def device(self, y_hi=None, x=None, core=None, y_lo=None, z=None):
        y_hi = self.y_hi if y_hi is None else y_hi
        x = self.x if x is None else x
        core = self.core if core is None else core
        y_lo = self.y_lo if y_lo is None else y_lo
        z = self.z if z is None else z
        return (y_hi * 8 + x * 2 + core, y_lo * 4 + z)

    def along(self, axis, step):
        if axis == "x":
            at = (self.x + step) % 4
            return self.device(x=at), at
        if axis == "z":
            at = (self.z + step) % 4
            return self.device(z=at), at
        at = (self.y + step) % 4
        return self.device(y_hi=at // 2, y_lo=at % 2), (at % 2) * 2 + at // 2


def greet(place):
    barrier = pltpu.get_barrier_semaphore()
    count = 1
    pl.semaphore_signal(barrier, inc=1, device_id=place.device(core=1 - place.core), device_id_type=MESH)
    for axis in ("x", "y", "z"):
        for step in (1, 2, 3):
            pl.semaphore_signal(barrier, inc=1, device_id=place.along(axis, step)[0], device_id_type=MESH)
            count += 1
    for step in (1, 2, 3):
        target = place.device(y_hi=1 - place.y_hi, x=(place.x + step) % 4)
        pl.semaphore_signal(barrier, inc=1, device_id=target, device_id_type=MESH)
        count += 1
    pl.semaphore_wait(barrier, count)


def lhs_block(at_ref, part, slot, second):
    if part == 0:
        block = at_ref[second // 2, :, second % 2, slot]
    elif part == 1:
        block = at_ref[slot // 2, second, slot % 2]
    else:
        block = at_ref[:, slot, :, second]
    return block.reshape(-1, block.shape[-1])


def chunk_product(at_ref, g_ref, part, slot, tile, width, emit):
    depth = at_ref.shape[4]
    right = g_ref[:, tile * LANES : (tile + width) * LANES]
    group = 1 if depth >= 64 else 4
    for base in range(0, 4, group):
        left = [lhs_block(at_ref, part, slot, base + i) for i in range(group)]
        left = left[0] if group == 1 else jnp.concatenate(left, axis=0)
        product = jnp.dot(left, right, preferred_element_type=jnp.float32)
        for column in range(width):
            emit(
                tile + column,
                base,
                group,
                product[:, column * LANES : (column + 1) * LANES].reshape(group, 4, depth, LANES),
            )


class Reduction:
    def __init__(self, place, index, shares, refs, sems):
        self.place, self.index, self.refs, self.sems = place, index, refs, sems
        self.bounds, start = [], 0
        for share in shares:
            self.bounds.append((start, start + share))
            start += share

    def load(self):
        r, s, i, core = self.refs, self.sems, self.index, self.place.core
        tokens = r["at_in"].shape[-1]
        half = r["g"].shape[1]
        mine = pl.ds(pl.multiple_of(core * half, LANES), half)
        other = pl.ds(pl.multiple_of((1 - core) * half, LANES), half)
        partner = self.place.device(core=1 - core)
        local = [
            pltpu.make_async_copy(r["at_in"], r["at"].at[:, :, :, :, :, :tokens], s["local"].at[i, 0]),
            pltpu.make_async_copy(r["g_in"].at[:, mine], r["g"].at[:tokens], s["local"].at[i, 1]),
        ]
        remote = [
            pltpu.make_async_remote_copy(
                r["at_in"], r["at"].at[:, :, :, :, :, tokens:], s["ex_send"].at[i, 0], s["ex_recv"].at[i, 0],
                device_id=partner, device_id_type=MESH,
            ),
            pltpu.make_async_remote_copy(
                r["g_in"].at[:, other], r["g"].at[tokens:], s["ex_send"].at[i, 1], s["ex_recv"].at[i, 1],
                device_id=partner, device_id_type=MESH,
            ),
        ]
        for copy in remote + local:
            copy.start()
        self.loads = (local, remote)

    def loaded(self):
        for copy in self.loads[0]:
            copy.wait()
        for copy in self.loads[1]:
            copy.wait_recv()

    def copy(self, part, stage, step):
        r, s, i = self.refs, self.sems, self.index
        low, high = self.bounds[part]
        device, slot = self.place.along(ORDERS[part][stage], step)
        if stage == 0:
            source = r["s1"].at[step - 1, low:high]
            target = r["r1"].at[step - 1, low:high]
        elif stage == 1:
            source = r["r1"].at[0, low:high, slot]
            target = r["r2"].at[step - 1, low:high]
        else:
            source = r["r2"].at[0, low:high, slot]
            target = r["r3"].at[step - 1, low:high]
        return pltpu.make_async_remote_copy(
            source, target, s["send"].at[i, part, stage, step - 1], s["recv"].at[i, part, stage, step - 1],
            device_id=device, device_id_type=MESH,
        )

    def first(self):
        r = self.refs
        for part in range(3):
            low, high = self.bounds[part]

            def one(step, _, part=part, low=low, high=high):
                slot = self.place.along(ORDERS[part][0], step)[1]

                def emit(tile, base, group, value):
                    r["s1"][step - 1, tile, base : base + group] = value.astype(jnp.bfloat16)

                for tile in range(low, high, 2):
                    chunk_product(r["at"], r["g"], part, slot, tile, min(2, high - tile), emit)
                self.copy(part, 0, step).start()
                return _

            lax.fori_loop(1, 4, one, 0)

    def second(self):
        r = self.refs
        for part in range(3):
            low, high = self.bounds[part]
            slot = self.place.along(ORDERS[part][0], 0)[1]
            for step in (1, 2, 3):
                self.copy(part, 0, step).wait_recv()

            def emit(tile, base, group, value):
                at = slice(base, base + group)
                total = value
                for i in range(3):
                    total = total + r["r1"][i, tile, at].astype(jnp.float32)
                r["r1"][0, tile, at] = total.astype(jnp.bfloat16)

            for tile in range(low, high, 2):
                chunk_product(r["at"], r["g"], part, slot, tile, min(2, high - tile), emit)
            for step in (1, 2, 3):
                self.copy(part, 1, step).start()

    def third(self):
        r = self.refs
        for part in range(3):
            low, high = self.bounds[part]
            slot = self.place.along(ORDERS[part][1], 0)[1]
            for step in (1, 2, 3):
                self.copy(part, 1, step).wait_recv()

            for tile in range(low, high):
                total = r["r1"][0, tile, slot].astype(jnp.float32)
                for i in range(3):
                    total = total + r["r2"][i, tile].astype(jnp.float32)
                r["r2"][0, tile] = total.astype(jnp.bfloat16)
            for step in (1, 2, 3):
                self.copy(part, 2, step).start()

    def mine(self):
        return self.place.y_hi * 4 + self.place.x

    def gather_copy(self, y_hi, x, slot):
        r, s, i, place = self.refs, self.sems, self.index, self.place
        block = r["ag"].at[slot, place.core]
        return pltpu.make_async_remote_copy(
            block, block, s["ag_send"].at[i, y_hi * 4 + x], s["ag_recv"].at[i, slot],
            device_id=place.device(y_hi=y_hi, x=x), device_id_type=MESH,
        )

    def others(self):
        place = self.place
        for y_step in (0, 1):
            y_hi = (place.y_hi + y_step) % 2
            for x_step in range(4):
                if y_step or x_step:
                    yield y_hi, (place.x + x_step) % 4

    def fourth(self):
        r = self.refs
        for part in range(3):
            low, high = self.bounds[part]
            slot = self.place.along(ORDERS[part][2], 0)[1]
            for step in (1, 2, 3):
                self.copy(part, 2, step).wait_recv()
            for tile in range(low, high):
                total = r["r2"][0, tile, slot].astype(jnp.float32)
                for i in range(3):
                    total = total + r["r3"][i, tile].astype(jnp.float32)
                r["ag"][self.mine(), self.place.core, tile] = total.astype(jnp.bfloat16)
        for y_hi, x in self.others():
            self.gather_copy(y_hi, x, self.mine()).start()

    def cross_copy(self):
        r, s, i, core = self.refs, self.sems, self.index, self.place.core
        block = r["ag"].at[:, core]
        return pltpu.make_async_remote_copy(
            block, block, s["cross"].at[i, 0], s["cross"].at[i, 1],
            device_id=self.place.device(core=1 - core), device_id_type=MESH,
        )

    def fifth(self):
        for y_hi, x in self.others():
            self.gather_copy(y_hi, x, y_hi * 4 + x).wait_recv()
        self.cross_copy().start()

    def out_copy(self):
        return pltpu.make_async_copy(self.refs["ag"], self.refs["out"], self.sems["local"].at[self.index, 2])

    def sixth(self):
        self.cross_copy().wait_recv()
        self.out_copy().start()

    def finish(self):
        self.out_copy().wait()
        self.cross_copy().wait_send()
        for copy in self.loads[1]:
            copy.wait_send()
        for y_hi, x in self.others():
            self.gather_copy(y_hi, x, self.mine()).wait_send()
        for part in range(3):
            for stage in range(3):
                for step in (1, 2, 3):
                    self.copy(part, stage, step).wait_send()


def gradient_kernel(*refs):
    count = len(MATRICES)
    names = ("at_in", "g_in", "out", "at", "g", "s1", "r1", "r2", "r3", "ag")
    groups = {name: refs[i * count : (i + 1) * count] for i, name in enumerate(names)}
    sem_names = ("local", "ex_send", "ex_recv", "send", "recv", "ag_send", "ag_recv", "cross")
    sems = dict(zip(sem_names, refs[len(names) * count :]))
    place = Place()
    work = [
        Reduction(place, i, shares, {name: groups[name][i] for name in names}, sems)
        for i, (_, shares) in enumerate(MATRICES)
    ]
    greet(place)
    for one in work:
        one.load()
    stages = ("first", "second", "third", "fourth", "fifth", "sixth")
    for turn in range(count + len(stages) - 1):
        for lag, stage in enumerate(stages):
            if 0 <= turn - lag < count:
                if lag == 0:
                    work[turn].loaded()
                getattr(work[turn - lag], stage)()
    for one in work:
        one.finish()


def reduce_gradients(pairs):
    lefts, rights, outs, scratch = [], [], [], {n: [] for n in ("at", "g", "s1", "r1", "r2", "r3", "ag")}
    bf16 = jnp.bfloat16
    flops = 0
    for activation, gradient in pairs:
        tokens, k = activation.shape
        n = gradient.shape[1]
        depth, tiles = k // 64, n // 2 // LANES
        flops += 2 * tokens * k * n
        lefts.append(activation.T.reshape(2, 4, 2, 4, depth, tokens))
        rights.append(gradient)
        outs.append(jax.ShapeDtypeStruct((8, 2, tiles, depth, LANES), bf16))
        scratch["at"].append(pltpu.VMEM((2, 4, 2, 4, depth, 2 * tokens), bf16))
        scratch["g"].append(pltpu.VMEM((2 * tokens, n // 2), bf16))
        scratch["s1"].append(pltpu.VMEM((3, tiles, 4, 4, depth, LANES), bf16))
        scratch["r1"].append(pltpu.VMEM((3, tiles, 4, 4, depth, LANES), bf16))
        scratch["r2"].append(pltpu.VMEM((3, tiles, 4, depth, LANES), bf16))
        scratch["r3"].append(pltpu.VMEM((3, tiles, depth, LANES), bf16))
        scratch["ag"].append(pltpu.VMEM((8, 2, tiles, depth, LANES), bf16))
    count = len(pairs)
    sem = pltpu.SemaphoreType.DMA
    results = pl.pallas_call(
        gradient_kernel,
        out_shape=outs,
        in_specs=[ANY] * (2 * count),
        out_specs=[ANY] * count,
        scratch_shapes=[one for group in scratch.values() for one in group]
        + [
            sem((count, 3)),
            sem((count, 2)),
            sem((count, 2)),
            sem((count, 3, 3, 3)),
            sem((count, 3, 3, 3)),
            sem((count, 8)),
            sem((count, 8)),
            sem((count, 2)),
        ],
        compiler_params=pltpu.CompilerParams(
            collective_id=0, has_side_effects=True, vmem_limit_bytes=58 * 2**20
        ),
        cost_estimate=pl.CostEstimate(flops=flops, bytes_accessed=40 * 2**20, transcendentals=0),
        name="gradient_sums",
    )(*lefts, *rights)
    finished = []
    for value in results:
        rows, cores, tiles, depth, lanes = value.shape
        value = value.transpose(0, 3, 1, 2, 4).reshape(rows * depth, cores * tiles * lanes)
        finished.append(value.astype(jnp.float32))
    return finished


def from_partner(value, axis):
    pairs = [(source, source ^ 1) for source in range(lax.axis_size(axis))]
    return lax.ppermute(value, axis, pairs)


def normalize(rows, gain, shift):
    mean_row = jnp.mean(rows, axis=-1, keepdims=True)
    centered = rows - mean_row
    variance = jnp.mean(centered * centered, axis=-1, keepdims=True)
    return centered * lax.rsqrt(variance + EPSILON) * gain + shift


def norm_backward(rows, gain, shift, gradient):
    unused_value, pullback = jax.vjp(normalize, rows, gain, shift)
    return pullback(gradient)


def project(activation, weight):
    return jnp.einsum("...k,kn->...n", activation, weight, preferred_element_type=jnp.float32)


def project_back(gradient, weight):
    return jnp.einsum("...n,kn->...k", gradient, weight, preferred_element_type=jnp.float32)


def score_rows(queries, key_rows, visible):
    scores = jnp.einsum("bqhe,bkhe->bhqk", queries, key_rows, preferred_element_type=jnp.float32)
    return jnp.where(visible, scores * queries.shape[-1] ** (-0.5), MASKED_SCORE)


def attend_forward(queries, key_rows, value_rows, visible):
    scores = score_rows(queries, key_rows, visible)
    row_max = jnp.max(scores, axis=-1, keepdims=True)
    weights = jnp.exp(scores - row_max)
    row_total = jnp.sum(weights, axis=-1, keepdims=True)
    probability = (weights / row_total).astype(jnp.bfloat16)
    context = jnp.einsum("bhqk,bkhe->bqhe", probability, value_rows, preferred_element_type=jnp.float32)
    return (context.astype(jnp.bfloat16), row_max + jnp.log(row_total))


def attend_backward(queries, key_rows, value_rows, visible, log_total, context_grad):
    scale_factor = queries.shape[-1] ** (-0.5)
    probability = jnp.exp(score_rows(queries, key_rows, visible) - log_total)
    prob_grad = jnp.einsum("bqhe,bkhe->bhqk", context_grad, value_rows, preferred_element_type=jnp.float32)
    row_delta = jnp.sum(probability * prob_grad, axis=-1, keepdims=True)
    score_grad = (probability * (prob_grad - row_delta)).astype(jnp.bfloat16)
    low_prob = probability.astype(jnp.bfloat16)
    query_grad = jnp.einsum("bhqk,bkhe->bqhe", score_grad, key_rows, preferred_element_type=jnp.float32)
    key_grad = jnp.einsum("bhqk,bqhe->bkhe", score_grad, queries, preferred_element_type=jnp.float32)
    value_grad = jnp.einsum("bhqk,bqhe->bkhe", low_prob, context_grad, preferred_element_type=jnp.float32)
    return (query_grad * scale_factor, key_grad * scale_factor, value_grad)


def to_positions(rows):
    width = rows.shape[-1]
    blocks = rows.reshape(2, 16, 8, width).swapaxes(0, 1)
    blocks = lax.all_to_all(blocks, "ta", split_axis=0, concat_axis=0, tiled=True)
    return blocks.reshape(8, 2, 16, width).swapaxes(0, 1).reshape(2, 128, width)


def to_frames(rows):
    width = rows.shape[-1]
    blocks = rows.reshape(2, 8, 16, width).swapaxes(0, 1).reshape(16, 2, 8, width)
    blocks = lax.all_to_all(blocks, "ta", split_axis=0, concat_axis=0, tiled=True)
    return blocks.swapaxes(0, 1).reshape(2, 128, width)


def body(
    big_tokens,
    small_tokens,
    big_actions,
    small_actions,
    big_order,
    small_order,
    small_live,
    action_table,
    norm1_gain,
    norm1_bias,
    spatial_qkv,
    spatial_out,
    spatial_out_bias,
    norm2_gain,
    norm2_bias,
    temporal_qkv,
    temporal_out,
    temporal_out_bias,
    norm3_gain,
    norm3_bias,
    ffn_in,
    ffn_in_bias,
    ffn_out,
    ffn_out_bias,
    big_cotangent,
    small_cotangent,
):
    f32, bf16 = jnp.float32, jnp.bfloat16
    width = big_tokens.shape[2]
    heads = width // HEAD_DIM
    ta = lax.axis_index("ta")
    frame = ta // 2
    gain_one, shift_one = norm1_gain.astype(f32), norm1_bias.astype(f32)
    gain_two, shift_two = norm2_gain.astype(f32), norm2_bias.astype(f32)
    gain_three, shift_three = norm3_gain.astype(f32), norm3_bias.astype(f32)

    def merge(big, small):
        return jnp.concatenate([big.reshape(1, 128, -1), small.reshape(1, 128, -1)], axis=0)

    alive = jnp.repeat(small_live.astype(f32), 32)
    alive = jnp.concatenate([jnp.ones((128,), f32), alive]).reshape(2, 128, 1)
    actions = jnp.concatenate([big_actions, small_actions], axis=0)
    chosen = jnp.arange(8)[None, :] == frame
    action_now = jnp.sum(jnp.where(chosen, actions, 0), axis=1)
    pick = action_now[:, None] == jnp.arange(8)[None, :]
    embedding = jnp.dot(pick.astype(bf16), action_table, preferred_element_type=f32)
    tokens = merge(big_tokens, small_tokens).astype(f32)
    embedded = jnp.concatenate([jnp.repeat(embedding[:1], 128, axis=0), jnp.repeat(embedding[1:], 32, axis=0)], axis=0)
    resid_zero = tokens + embedded.reshape(2, 128, width)
    slots = jnp.arange(128) // 32
    same_slot = slots[:, None] == jnp.concatenate([slots, slots])[None, :]
    spatial_mask = jnp.stack([jnp.ones_like(same_slot), same_slot])[:, None]
    mine = jnp.arange(4)[:, None] == ta // 4
    small_rank = jnp.sum(jnp.where(mine, small_order, 0), axis=0)
    rank = jnp.stack([big_order[0], small_rank], axis=1)
    rank = jnp.repeat(rank, 8, axis=1).reshape(128)
    spot = jnp.arange(128) % 16
    temporal_mask = (spot[:, None] == spot[None, :]) & (rank[None, :] <= rank[:, None])
    temporal_mask = temporal_mask[None, None]

    def split_heads(rows):
        return rows.reshape(rows.shape[0], rows.shape[1], heads, HEAD_DIM)

    normed_one = normalize(resid_zero, gain_one, shift_one).astype(bf16)
    packed_one = project(normed_one, spatial_qkv).astype(bf16)
    far = from_partner(packed_one[:, :, width:], "ta")
    joined = jnp.concatenate([packed_one[:, :, width:], far], axis=1)
    q1, k1, v1 = split_heads(packed_one[:, :, :width]), split_heads(joined[:, :, :width]), split_heads(joined[:, :, width:])
    context_one, log_one = attend_forward(q1, k1, v1, spatial_mask)
    context_one = context_one.reshape(2, 128, width)
    resid_one = resid_zero + project(context_one, spatial_out) + spatial_out_bias.astype(f32)
    normed_two = normalize(resid_one, gain_two, shift_two).astype(bf16)
    arranged = to_positions(normed_two)
    packed_two = project(arranged, temporal_qkv).astype(bf16)
    q2, k2, v2 = (split_heads(packed_two[:, :, i * width : (i + 1) * width]) for i in range(3))
    context_two, log_two = attend_forward(q2, k2, v2, temporal_mask)
    context_two = to_frames(context_two.reshape(2, 128, width))
    resid_two = resid_one + project(context_two, temporal_out) + temporal_out_bias.astype(f32)
    normed_three = normalize(resid_two, gain_three, shift_three).astype(bf16)
    hidden = project(normed_three, ffn_in) + ffn_in_bias.astype(f32)
    activated = jax.nn.gelu(hidden).astype(bf16)
    result = (resid_two + project(activated, ffn_out) + ffn_out_bias.astype(f32)) * alive
    result = result.astype(bf16)

    grad_three = merge(big_cotangent, small_cotangent).astype(f32) * alive
    grad_three_low = grad_three.astype(bf16)
    gelu_value, gelu_pull = jax.vjp(jax.nn.gelu, hidden)
    hidden_grad = gelu_pull(project_back(grad_three_low, ffn_out))[0]
    hidden_low = hidden_grad.astype(bf16)
    rows_grad, gain_three_grad, shift_three_grad = norm_backward(
        resid_two, gain_three, shift_three, project_back(hidden_low, ffn_in)
    )
    grad_two = grad_three + rows_grad
    grad_two_low = grad_two.astype(bf16)
    context_grad = to_positions(project_back(grad_two_low, temporal_out).astype(bf16))
    grads = attend_backward(q2, k2, v2, temporal_mask, log_two, split_heads(context_grad))
    packed_two_grad = jnp.concatenate([g.reshape(2, 128, width) for g in grads], axis=-1).astype(bf16)
    normed_two_grad = to_frames(project_back(packed_two_grad, temporal_qkv).astype(bf16)).astype(f32)
    rows_grad, gain_two_grad, shift_two_grad = norm_backward(resid_one, gain_two, shift_two, normed_two_grad)
    grad_one = grad_two + rows_grad
    grad_one_low = grad_one.astype(bf16)
    context_grad = project_back(grad_one_low, spatial_out).astype(bf16)
    query_grad, key_grad, value_grad = attend_backward(q1, k1, v1, spatial_mask, log_one, split_heads(context_grad))
    key_value = jnp.concatenate([key_grad.reshape(2, 256, width), value_grad.reshape(2, 256, width)], axis=-1)
    far = from_partner(key_value[:, 128:].astype(bf16), "ta").astype(f32)
    packed_one_grad = jnp.concatenate([query_grad.reshape(2, 128, width), key_value[:, :128] + far], axis=-1).astype(bf16)
    rows_grad, gain_one_grad, shift_one_grad = norm_backward(
        resid_zero, gain_one, shift_one, project_back(packed_one_grad, spatial_qkv)
    )
    grad_zero = grad_one + rows_grad
    frame_sums = jnp.concatenate(
        [jnp.sum(grad_zero[0], axis=0, keepdims=True), jnp.sum(grad_zero[1].reshape(4, 32, width), axis=1)], axis=0
    )
    table_grad = jnp.sum(jnp.where(pick[:, :, None], frame_sums[:, None, :], 0.0), axis=0)

    def rows_sum(value):
        return jnp.sum(value, axis=(0, 1)).reshape(-1, width)

    small = jnp.concatenate(
        [
            table_grad,
            gain_one_grad[None],
            shift_one_grad[None],
            rows_sum(grad_one),
            gain_two_grad[None],
            shift_two_grad[None],
            rows_sum(grad_two),
            gain_three_grad[None],
            shift_three_grad[None],
            rows_sum(hidden_grad),
            rows_sum(grad_three),
        ],
        axis=0,
    )
    small = lax.psum(small, ("ta", "col"))

    def flat(value):
        return value.reshape(256, value.shape[-1])

    g_fout, g_fin, g_tout, g_tqkv, g_sout, g_sqkv = reduce_gradients(
        [
            (flat(activated), flat(grad_three_low)),
            (flat(normed_three), flat(hidden_low)),
            (flat(context_two), flat(grad_two_low)),
            (flat(arranged), flat(packed_two_grad)),
            (flat(context_one), flat(grad_one_low)),
            (flat(normed_one), flat(packed_one_grad)),
        ]
    )
    return (
        result[0].reshape(1, 128, width),
        result[1].reshape(4, 32, width),
        grad_zero[0].reshape(1, 128, width),
        grad_zero[1].reshape(4, 32, width),
        small[:8],
        small[8],
        small[9],
        g_sqkv,
        g_sout,
        small[10],
        small[11],
        small[12],
        g_tqkv,
        g_tout,
        small[13],
        small[14],
        small[15],
        g_fin,
        small[16:20].reshape(-1),
        g_fout,
        small[20],
    )


def solution(mesh):
    spread, by_col = P("col", "ta", None), P("col", None)
    return jax.shard_map(
        body,
        mesh=mesh,
        in_specs=(spread, spread, by_col, by_col, by_col, by_col, P("col")) + (P(),) * 17 + (spread, spread),
        out_specs=(spread,) * 4
        + (P(),) * 3
        + (by_col, by_col, P(), P(), P(), by_col, by_col, P(), P(), P(), by_col, P(), by_col, P()),
        check_vma=False,
    )
```

time: 989 us -> 436 us (0.44)
  blocking collectives: 337 us -> 0 us
  local copies, waits for them, and re-layouts: 294 us -> 109 us
  Pallas kernels: 0 us -> 126 us
  matrix products: 183 us -> 70.3 us
  starting transfers between devices: 61.4 us -> 28.8 us
    psum x1 -> x0, blocking collectives: 337 us -> none  [body(): lax.psum((table_terms[0] + table_terms[1], gain1_terms[0] + gain1_terms[1...]
    reshape x37 -> x13, local copies, waits for them, and re-layouts: 177 us -> 15.4 us  [the longest x2 4.5 us: flat(): return value.reshape(256, value.shape[-1])]
    pallas_call x0 -> x1, Pallas kernels: none -> 126 us  [reduce_gradients(): pl.pallas_call(gradient_kernel, out_shape=outs, in_specs=[ANY] * (2 * cou...]
    dot_general x39 -> x13, matrix products: 102 us -> 22.7 us  [the longest x2 4.91 us: attend_backward(): jnp.einsum('bhqk,bqhe->bkhe', low_prob, context_grad, preferred_element_t...]
    unnamed x341 -> x173, local copies, waits for them, and re-layouts: 56.5 us -> 13.1 us
    all_gather x1 -> x0, waiting for transfers between devices: 42.9 us -> none  [one_gather(): lines, at, finished = (lax.all_gather(ravelled, axis), 0, [])]
    all_to_all x8 -> x4, starting transfers between devices: 59.5 us -> 25.8 us  [the longest x2 13.2 us: to_positions(): lax.all_to_all(blocks, 'ta', split_axis=0, concat_axis=0, tiled=True)]
    all_to_all x8 -> x4, waiting for transfers between devices: 1.24 us -> 21.2 us  [the longest x2 10.8 us: to_positions(): lax.all_to_all(blocks, 'ta', split_axis=0, concat_axis=0, tiled=True)]
  transfers between devices with their start and end apart: 13 -> 7, of which waited for: 2 -> 5; matrix products, arithmetic and copies ran while one was open for 35% -> 20% of each run, Pallas kernels for 0% -> 29%
where the time goes in v1:
time: 436 us; the launch traced here: 428 us
  Pallas kernels  126 us (29%)
  local copies, waits for them, and re-layouts  109 us (25%)
  matrix products  70.3 us (16%)
  other arithmetic  39.3 us (9%)
  waiting for transfers between devices  39 us (9%)
  starting transfers between devices  28.8 us (7%)
  between operations  15.6 us (4%)
    pallas_call x1, Pallas kernels, reduce_gradients(): pl.pallas_call(gradient_kernel, out_shape=outs, in_specs=[ANY] * (2 * cou...  126 us
    dot_general x6, matrix products, project(): jnp.einsum('...k,kn->...n', activation, weight, preferred_element_type=jn...  25 us
    dot_general x6, matrix products, project_back(): jnp.einsum('...n,kn->...k', gradient, weight, preferred_element_type=jnp....  22.6 us
    convert_element_type x12, local copies, waits for them, and re-layouts, reduce_gradients(): finished.append(value.astype(jnp.float32))  19.8 us
    psum x1, waiting for transfers between devices, body(): small = lax.psum(small, ('ta', 'col'))  16.3 us
    all_to_all x2, starting transfers between devices, to_positions(): lax.all_to_all(blocks, 'ta', split_axis=0, concat_axis=0, tiled=True)  13.2 us
    unnamed x173, local copies, waits for them, and re-layouts  13.1 us
    concatenate x6, local copies, waits for them, and re-layouts, body(): jnp.concatenate([g.reshape(2, 128, width) for g in grads], axis=-1)  13.1 us
  transfers between devices with their start and end apart: 7, of which 5 were waited for; matrix products, arithmetic and copies ran while one was open for 20% of the time, Pallas kernels for 29%

profile of v1, /device:TPU:1, one launch (start us, length us, event | category | flops | bytes accessed | tf_op | source)
XLA Modules:
  0.0 428.3 jit_solution(16983946376117959930)
XLA Ops:
  12.1 2.1 copy-done.78
  14.1 1.9 fusion.27
  21.2 2.7 pad_maximum_fusion.3
  26.7 2.6 fusion.147
  31.4 2.1 fusion.99
  35.7 7.7 %all-to-all-start = ((bf16[16,2,8,1024]{3,2,1,0:T(8,128)(2,1)}), bf16[16,2,8,1024]{3,2,1,0:T(8,128)(2,1)}, u32[]{:S(2)}, u32[]{:S(2)}) async-start(bf16[16,2,8,1024]{3,2,1,0:T(8,128)(2,1)} %copy_bitcast_fusion.2), calls=%async_computation | async-start | bytes 1048576 | tf_op jit(solution)/shard_map/all_to_all | solution.py:408
  44.1 10.8 %all-to-all-done = bf16[16,2,8,1024]{3,2,1,0:T(8,128)(2,1)} async-done(((bf16[16,2,8,1024]{3,2,1,0:T(8,128)(2,1)}), bf16[16,2,8,1024]{3,2,1,0:T(8,128)(2,1)}, u32[]{:S(2)}, u32[]{:S(2)}) %all-to-all-start) | async-done | bytes 524320 | tf_op jit(solution)/shard_map/all_to_all | solution.py:408
  55.9 4.8 %fusion.30 = bf16[2,128,3072]{2,1,0:T(8,128)(2,1)S(1)} fusion(bf16[2,128,1024]{2,1,0:T(8,128)(2,1)S(1)} %bitcast.331, bf16[1024,3072]{1,0:T(8,128)(2,1)} %param.41), kind=kOutput, calls=%fused_computation.35 | convolution fusion | flops 1611399168 | bytes 8388608 | tf_op jit(solution)/shard_map/...k,kn->...n/dot_general | solution.py:370
  61.9 2.0 copy.142
  63.9 2.0 copy.144
  66.0 2.0 copy.145
  68.0 1.8 fusion.149
  72.4 2.7 copy.147
  75.2 2.7 reshape_reshape.15
  77.8 1.9 copy.148
  79.7 5.4 %all-to-all-start.1 = ((bf16[16,2,8,1024]{3,2,1,0:T(8,128)(2,1)}), bf16[16,2,8,1024]{3,2,1,0:T(8,128)(2,1)}, u32[]{:S(2)}, u32[]{:S(2)}) async-start(bf16[16,2,8,1024]{3,2,1,0:T(8,128)(2,1)} %bitcast.334), calls=%async_computation.1 | async-start | bytes 1048576 | tf_op jit(solution)/shard_map/all_to_all | solution.py:415
  87.8 1.9 fusion.106.refs_6_
  89.7 6.8 %all-to-all-done.1 = bf16[16,2,8,1024]{3,2,1,0:T(8,128)(2,1)} async-done(((bf16[16,2,8,1024]{3,2,1,0:T(8,128)(2,1)}), bf16[16,2,8,1024]{3,2,1,0:T(8,128)(2,1)}, u32[]{:S(2)}, u32[]{:S(2)}) %all-to-all-start.1) | async-done | bytes 524320 | tf_op jit(solution)/shard_map/all_to_all | solution.py:415
  96.5 1.8 fusion.150
  98.9 8.5 %multiply_convert_fusion.1 = (bf16[2,128,4096]{2,1,0:T(8,128)(2,1)}, f32[2,128,4096]{2,1,0:T(8,128)S(1)}) fusion(f32[4096]{0:T(1024)S(1)} %convert_element_type.233, bf16[2,128,1024]{2,1,0:T(8,128)(2,1)S(1)} %add_convert_fusion, bf16[1024,4096]{1,0:T(8,128)(2,1)} %param.46), kind=kOutput, calls=%fused_computation.30 | convolution fusion | flops 2157969408 | bytes 15220736 | tf_op jit(solution)/shard_map/...k,kn->...n/dot_general | solution.py:370
  107.5 7.7 %fusion.142 = (f32[4096]{0:T(1024)S(1)}, bf16[2,128,4096]{2,1,0:T(8,128)(2,1)S(1)}) fusion(f32[2,128,4096]{2,1,0:T(8,128)S(1)} %get-tuple-element.88, bf16[4096,1024]{1,0:T(8,128)(2,1)S(1)} %bitcast.379, f32[2,128]{1,0:T(2,128)S(1)} %get-tuple-element.78, bf16[1,128,1024]{2,1,0:T(8,128)(2,1)S(1)} %bitcast.323, bf16[1,128,1024]{2,1,0:T(8,128)(2,1)S(1)} %copy-done.42), kind=kOutput, calls=%fused_computation.204 | convolution fusion | flops 2170548224 | bytes 15221760 | tf_op jit(solution)/shard_map/...n,kn->...k/dot_general | solution.py:374
  115.2 3.2 multiply_reduce_fusion.2
  121.6 5.5 %all-to-all-start.2 = ((bf16[16,2,8,1024]{3,2,1,0:T(8,128)(2,1)}), bf16[16,2,8,1024]{3,2,1,0:T(8,128)(2,1)}, u32[]{:S(2)}, u32[]{:S(2)}) async-start(bf16[16,2,8,1024]{3,2,1,0:T(8,128)(2,1)} %bitcast.294), calls=%async_computation.2 | async-start | bytes 1048576 | tf_op jit(solution)/shard_map/all_to_all | solution.py:408
  127.1 2.2 maximum_convert_fusion
  132.5 2.1 copy.171
  134.6 2.5 copy.166
  137.0 2.0 copy.167
  141.2 2.0 copy.151
  143.3 2.5 reshape_reshape.16
  145.8 2.8 copy.152
  148.6 2.8 convolution_convert_fusion
  156.8 4.8 %fusion.87 = bf16[2,128,1024]{2,1,0:T(8,128)(2,1)S(1)} fusion(bf16[1024,3072]{1,0:T(8,128)(2,1)} %param.41, bf16[2,128,1024]{2,1,0:T(8,128)(2,1)S(1)} %copy-done.62, bf16[2,128,1024]{2,1,0:T(8,128)(2,1)} %copy.158, bf16[2,128,1024]{2,1,0:T(8,128)(2,1)S(1)} %copy.157), kind=kOutput, calls=%fused_computation.97 | convolution fusion | flops 1615593472 | bytes 8388608 | tf_op jit(solution)/shard_map/...n,kn->...k/dot_general | solution.py:374
  162.4 7.3 %all-to-all-start.3 = ((bf16[16,2,8,1024]{3,2,1,0:T(8,128)(2,1)}), bf16[16,2,8,1024]{3,2,1,0:T(8,128)(2,1)S(1)}, u32[]{:S(2)}, u32[]{:S(2)}) async-start(bf16[16,2,8,1024]{3,2,1,0:T(8,128)(2,1)} %bitcast.45), calls=%async_computation.3 | async-start | bytes 1048576 | tf_op jit(solution)/shard_map/all_to_all | solution.py:415
  170.3 7.2 %fusion.82 = bf16[2,128,1024]{2,1,0:T(8,128)(2,1)} fusion(f32[2,128,1024]{2,1,0:T(8,128)S(1)} %copy-done.12, bf16[2,128,4096]{2,1,0:T(8,128)(2,1)} %get-tuple-element.87, bf16[4096,1024]{1,0:T(8,128)(2,1)} %param.48, f32[2,128]{1,0:T(2,128)S(1)} %get-tuple-element.78, f32[1024]{0:T(1024)S(1)} %copy-done.68), kind=kOutput, calls=%fused_computation.94 | convolution fusion | flops 2148532224 | bytes 12063744 | tf_op jit(solution)/shard_map/...k,kn->...n/dot_general | solution.py:370
  177.4 3.7 all-to-all-done.3
  185.8 3.6 multiply_reduce_fusion
  189.4 2.1 fusion.35
  192.9 2.0 convolution_multiply_fusion
  194.9 1.9 copy.163
  196.8 2.9 copy.164
  199.7 2.4 fusion.40
  204.1 1.7 copy.195
  205.8 2.8 reshape.641
  208.5 1.7 copy.194
  210.2 2.6 reshape.640
  214.5 2.7 reshape.639
  217.2 2.8 pad_maximum_fusion.1.refs_9_
  221.6 2.1 copy.165
  223.7 2.7 copy.196
  226.5 2.6 reshape.642
  229.2 1.9 fusion.39
  231.2 5.3 %fusion.136 = (f32[1024]{0:T(1024)S(1)}, f32[2,128]{1,0:T(2,128)S(1)}, f32[2,128,1024]{2,1,0:T(8,128)S(1)}) fusion(f32[1024]{0:T(1024)S(1)} %convert_element_type.214, f32[2,128,1024]{2,1,0:T(8,128)S(1)} %copy-done.8, f32[2,128]{1,0:T(2,128)S(1)} %get-tuple-element.74, bf16[1024,3072]{1,0:T(8,128)(2,1)} %param.36, bf16[2,128,2048]{2,1,0:T(8,128)(2,1)S(1)} %fusion.39, ...), kind=kOutput, calls=%fused_computation.199 | convolution fusion | flops 1615067904 | bytes 9971712 | tf_op jit(solution)/shard_map/...n,kn->...k/dot_general | solution.py:374
  240.1 1.9 concatenate.67
  243.1 2.0 copy.173
  245.2 2.3 pad_maximum_fusion.2.refs_11_
  247.5 126.1 %gradient_sums.1 = (bf16[8,2,4,64,128]{4,3,2,1,0:T(8,128)(2,1)}, bf16[8,2,16,16,128]{4,3,2,1,0:T(8,128)(2,1)}, bf16[8,2,4,16,128]{4,3,2,1,0:T(8,128)(2,1)}, bf16...) custom-call(bf16[2,4,2,4,64,256]{5,4,3,2,1,0:T(8,128)(2,1)} %bitcast.329,, ...), custom_call_target="tpu_custom_call" | custom-call | flops 8589934592 | bytes 41943040 | tf_op jit(solution)/shard_map/gradient_sums/pallas_call | solution.py:322
  373.6 2.9 convert_bitcast_fusion.1
  383.0 1.9 copy.184
  388.1 1.9 copy.186
  390.1 2.7 reshape.631
  392.8 4.5 %copy.187 = f32[8,64,2,4,128]{4,3,2,1,0:T(4,128)} copy(f32[8,64,2,4,128]{4,1,3,2,0:T(8,128)} %convert_bitcast_fusion) | data formatting | bytes 4194304 | tf_op jit(solution)/shard_map/convert_element_type | solution.py:348
  397.3 3.0 reshape.632
  400.3 16.3 %all-reduce.4.cloned.1.call-done = f32[21,1024]{1,0:T(8,128)} async-done(((f32[21,1024]{1,0:T(8,128)}), f32[21,1024]{1,0:T(8,128)}) %all-reduce.4.cloned.1.call-update) | async-done | bytes 86032 | tf_op jit(solution)/shard_map/psum | solution.py:554
  419.4 1.9 fusion.145
  (292 shorter events, 68.9 us)
Async XLA Ops:
  7.2 89.3 %copy-start = (bf16[1024,1024]{1,0:T(8,128)(2,1)S(1)}, bf16[1024,1024]{1,0:T(8,128)(2,1)}, u32[]{:S(2)}) copy-start(bf16[1024,1024]{1,0:T(8,128)(2,1)} %param.42) | copy-start | bytes 6291460
  7.2 4.4 %copy-start.54 = (bf16[4,32,1024]{2,1,0:T(8,128)(2,1)S(1)}, bf16[4,32,1024]{2,1,0:T(8,128)(2,1)}, u32[]{:S(2)}) copy-start(bf16[4,32,1024]{2,1,0:T(8,128)(2,1)} %param.27) | copy-start | bytes 786436
  7.2 4.4 %copy-start.55 = (bf16[1,128,1024]{2,1,0:T(8,128)(2,1)S(1)}, bf16[1,128,1024]{2,1,0:T(8,128)(2,1)}, u32[]{:S(2)}) copy-start(bf16[1,128,1024]{2,1,0:T(8,128)(2,1)} %param.26) | copy-start | bytes 786436
  10.6 3.5 copy-start.78
  11.8 4.3 %copy-start.6 = (f32[2,128,1024]{2,1,0:T(8,128)}, f32[2,128,1024]{2,1,0:T(8,128)S(1)}, u32[]{:S(2)}) copy-start(f32[2,128,1024]{2,1,0:T(8,128)S(1)} %get-tuple-element.51) | copy-start | bytes 3145732
  16.1 2.6 copy-start.69
  16.1 3.6 copy-start.70
  16.1 3.6 copy-start.71
  17.2 4.0 collective-permute-start
  26.7 2.6 copy-start.17
  29.3 2.1 copy-start.2
  29.3 2.1 copy-start.36
  31.3 2.1 copy-start.7
  31.3 2.1 copy-start.49
  34.3 9.1 %copy-start.74 = (s32[4,8]{1,0:T(4,128)S(1)}, s32[4,8]{1,0:T(4,128)}, u32[]{:S(2)}) copy-start(s32[4,8]{1,0:T(4,128)} %param.31) | copy-start | bytes 388
  34.3 9.2 %copy-start.77 = (s32[1,8]{1,0:T(1,128)S(1)}, s32[1,8]{1,0:T(1,128)}, u32[]{:S(2)}) copy-start(s32[1,8]{1,0:T(1,128)} %param.30) | copy-start | bytes 100
  34.3 9.4 %copy-start.79 = (s32[4]{0:T(128)S(1)}, s32[4]{0:T(128)}, u32[]{:S(2)}) copy-start(s32[4]{0:T(128)} %param.32) | copy-start | bytes 52
  35.7 19.2 %all-to-all-start = ((bf16[16,2,8,1024]{3,2,1,0:T(8,128)(2,1)}), bf16[16,2,8,1024]{3,2,1,0:T(8,128)(2,1)}, u32[]{:S(2)}, u32[]{:S(2)}) async-start(bf16[16,2,8,1024]{3,2,1,0:T(8,128)(2,1)} %copy_bitcast_fusion.2), calls=%async_computation | async-start | bytes 1048576 | tf_op jit(solution)/shard_map/all_to_all | solution.py:408
  55.9 4.8 %copy-start.47 = (bf16[2,8,16,1024]{3,2,1,0:T(8,128)(2,1)}, bf16[2,8,16,1024]{3,2,1,0:T(8,128)(2,1)S(1)}, u32[]{:S(2)}) copy-start(bf16[2,8,16,1024]{3,2,1,0:T(8,128)(2,1)S(1)} %copy.141) | copy-start | bytes 1572868
  68.0 3.1 copy-start.44
  75.2 9.9 %copy-start.72 = (bf16[1024]{0:T(1024)(128)(2,1)S(1)}, bf16[1024]{0:T(1024)(128)(2,1)}, u32[]{:S(2)}) copy-start(bf16[1024]{0:T(1024)(128)(2,1)} %param.43) | copy-start | bytes 6148
  75.2 10.0 %copy-start.65 = (bf16[4096]{0:T(1024)(128)(2,1)S(1)}, bf16[4096]{0:T(1024)(128)(2,1)}, u32[]{:S(2)}) copy-start(bf16[4096]{0:T(1024)(128)(2,1)} %param.47) | copy-start | bytes 24580
  75.2 12.6 %copy-start.41 = (bf16[4,32,1024]{2,1,0:T(8,128)(2,1)S(1)}, bf16[4,32,1024]{2,1,0:T(8,128)(2,1)}, u32[]{:S(2)}) copy-start(bf16[4,32,1024]{2,1,0:T(8,128)(2,1)} %param.51) | copy-start | bytes 786436
  79.7 16.8 %all-to-all-start.1 = ((bf16[16,2,8,1024]{3,2,1,0:T(8,128)(2,1)}), bf16[16,2,8,1024]{3,2,1,0:T(8,128)(2,1)}, u32[]{:S(2)}, u32[]{:S(2)}) async-start(bf16[16,2,8,1024]{3,2,1,0:T(8,128)(2,1)} %bitcast.334), calls=%async_computation.1 | async-start | bytes 1048576 | tf_op jit(solution)/shard_map/all_to_all | solution.py:415
  98.3 20.1 %copy-start.11 = (f32[2,128,1024]{2,1,0:T(8,128)}, f32[2,128,1024]{2,1,0:T(8,128)S(1)}, u32[]{:S(2)}) copy-start(f32[2,128,1024]{2,1,0:T(8,128)S(1)} %get-tuple-element.86) | copy-start | bytes 3145732
  98.6 8.8 %slice-start.2 = ((s8[8388608]{0:T(1024)(128)(4,1)}), s8[4194304]{0:T(1024)(128)(4,1)S(1)}, s32[]{:S(2)}) async-start(s8[8388608]{0:T(1024)(128)(4,1)} %bitcast.378), calls=%async_computation.7 | async-start | bytes 8388608
  98.9 8.5 %copy-start.48 = (bf16[2,128,1024]{2,1,0:T(8,128)(2,1)}, bf16[2,128,1024]{2,1,0:T(8,128)(2,1)S(1)}, u32[]{:S(2)}) copy-start(bf16[2,128,1024]{2,1,0:T(8,128)(2,1)S(1)} %add_convert_fusion) | copy-start | bytes 1572868
  98.9 8.5 %copy-start.42 = (bf16[1,128,1024]{2,1,0:T(8,128)(2,1)S(1)}, bf16[1,128,1024]{2,1,0:T(8,128)(2,1)}, u32[]{:S(2)}) copy-start(bf16[1,128,1024]{2,1,0:T(8,128)(2,1)} %param.50) | copy-start | bytes 786436
  98.9 8.5 %slice-start.3 = ((s8[8388608]{0:T(1024)(128)(4,1)}), s8[4194304]{0:T(1024)(128)(4,1)S(1)}, s32[]{:S(2)}) async-start(s8[8388608]{0:T(1024)(128)(4,1)} %bitcast.378), calls=%async_computation.8 | async-start | bytes 8388608
  98.9 16.2 %slice-start = ((s8[8388608]{0:T(1024)(128)(4,1)}), s8[4194304]{0:T(1024)(128)(4,1)S(1)}, s32[]{:S(2)}) async-start(s8[8388608]{0:T(1024)(128)(4,1)} %bitcast.376), calls=%async_computation.5 | async-start | bytes 8388608
  107.5 7.7 %slice-start.1 = ((s8[8388608]{0:T(1024)(128)(4,1)}), s8[4194304]{0:T(1024)(128)(4,1)S(1)}, s32[]{:S(2)}) async-start(s8[8388608]{0:T(1024)(128)(4,1)} %bitcast.376), calls=%async_computation.6 | async-start | bytes 8388608
  115.2 3.3 copy-start.80
  120.8 8.6 %copy-start.73 = (bf16[1024]{0:T(1024)(128)(2,1)S(1)}, bf16[1024]{0:T(1024)(128)(2,1)}, u32[]{:S(2)}) copy-start(bf16[1024]{0:T(1024)(128)(2,1)} %param.49) | copy-start | bytes 6148
  121.6 19.6 %all-to-all-start.2 = ((bf16[16,2,8,1024]{3,2,1,0:T(8,128)(2,1)}), bf16[16,2,8,1024]{3,2,1,0:T(8,128)(2,1)}, u32[]{:S(2)}, u32[]{:S(2)}) async-start(bf16[16,2,8,1024]{3,2,1,0:T(8,128)(2,1)} %bitcast.294), calls=%async_computation.2 | async-start | bytes 1048576 | tf_op jit(solution)/shard_map/all_to_all | solution.py:408
  127.1 7.4 %copy-start.46 = (bf16[2,128,4096]{2,1,0:T(8,128)(2,1)S(1)}, bf16[2,128,4096]{2,1,0:T(8,128)(2,1)}, u32[]{:S(2)}) copy-start(bf16[2,128,4096]{2,1,0:T(8,128)(2,1)} %get-tuple-element.87) | copy-start | bytes 6291460
  141.2 7.3 %copy-start.5 = (f32[2,16,128,128]{2,3,1,0:T(8,128)S(1)}, f32[2,16,128,128]{2,3,1,0:T(8,128)}, u32[]{:S(2)}) copy-start(f32[2,16,128,128]{2,3,1,0:T(8,128)} %copy-done.4) | copy-start | bytes 6291460
  148.5 2.8 copy-start.23
  148.6 2.8 copy-start.45
  154.1 2.5 copy-start.30
  154.5 2.3 copy-start.28
  161.6 8.7 %copy-start.12 = (f32[2,128,1024]{2,1,0:T(8,128)S(1)}, f32[2,128,1024]{2,1,0:T(8,128)}, u32[]{:S(2)}) copy-start(f32[2,128,1024]{2,1,0:T(8,128)} %copy-done.11) | copy-start | bytes 3145732
  161.6 8.7 %copy-start.68 = (f32[1024]{0:T(1024)S(1)}, f32[1024]{0:T(1024)}, u32[]{:S(2)}) copy-start(f32[1024]{0:T(1024)} %convert_element_type.235) | copy-start | bytes 12292
  162.4 18.7 %all-to-all-start.3 = ((bf16[16,2,8,1024]{3,2,1,0:T(8,128)(2,1)}), bf16[16,2,8,1024]{3,2,1,0:T(8,128)(2,1)S(1)}, u32[]{:S(2)}, u32[]{:S(2)}) async-start(bf16[16,2,8,1024]{3,2,1,0:T(8,128)(2,1)} %bitcast.45), calls=%async_computation.3 | async-start | bytes 1048576 | tf_op jit(solution)/shard_map/all_to_all | solution.py:415
  169.7 246.9 %all-reduce.4.cloned.1.call-start = ((), (), s32[]{:S(2)}) async-start(), calls=%async_computation.4 | async-start | bytes 196608 | tf_op jit(solution)/shard_map/psum | solution.py:554
  177.4 4.6 %copy-start.16 = (f32[2,128,1024]{2,1,0:T(8,128)S(1)}, f32[2,128,1024]{2,1,0:T(8,128)}, u32[]{:S(2)}) copy-start(f32[2,128,1024]{2,1,0:T(8,128)} %copy-done.15) | copy-start | bytes 3145732
  177.4 4.6 %copy-start.43 = (bf16[1,128,1024]{2,1,0:T(8,128)(2,1)S(1)}, bf16[1,128,1024]{2,1,0:T(8,128)(2,1)}, u32[]{:S(2)}) copy-start(bf16[1,128,1024]{2,1,0:T(8,128)(2,1)} %param.50) | copy-start | bytes 786436
  182.0 2.6 copy-start.50
  185.8 3.6 copy-start.3
  192.9 2.0 copy-start.9
  199.7 3.5 copy-start.60
  199.7 4.3 %copy-start.27 = (bf16[2,16,64,128]{3,2,1,0:T(8,128)(2,1)S(1)}, bf16[2,16,64,128]{3,2,1,0:T(8,128)(2,1)}, u32[]{:S(2)}) copy-start(bf16[2,16,64,128]{3,2,1,0:T(8,128)(2,1)} %convolution_convert_fusion) | copy-start | bytes 1572868
  202.2 6.4 %copy-start.31 = (bf16[2,16,64,128]{3,2,1,0:T(8,128)(2,1)S(1)}, bf16[2,16,64,128]{3,2,1,0:T(8,128)(2,1)}, u32[]{:S(2)}) copy-start(bf16[2,16,64,128]{3,2,1,0:T(8,128)(2,1)} %copy-done.30) | copy-start | bytes 1572868
  202.2 27.0 %collective-permute-start.1 = (bf16[2,128,2048]{2,1,0:T(8,128)(2,1)}, bf16[2,128,2048]{2,1,0:T(8,128)(2,1)}, u32[]{:S(2)}, u32[]{:S(2)}) collective-permute-start(bf16[2,128,2048]{2,1,0:T(8,128)(2,1)} %fusion.40), channel_id=1, source_target_pairs={{0,8},{8,0},{16,24},{24,16},{32,40},{40,32},{48,56},{56,48},{64,72... | collective-permute-start | bytes 3145736 | tf_op jit(solution)/shard_map/ppermute | solution.py:354
  205.8 7.1 %copy-start.29 = (bf16[2,16,64,128]{3,2,1,0:T(8,128)(2,1)S(1)}, bf16[2,16,64,128]{3,2,1,0:T(8,128)(2,1)}, u32[]{:S(2)}) copy-start(bf16[2,16,64,128]{3,2,1,0:T(8,128)(2,1)} %copy-done.28) | copy-start | bytes 1572868
  214.5 5.5 %copy-start.18 = (bf16[2,256,1024]{1,2,0:T(8,128)(2,1)S(1)}, bf16[2,256,1024]{1,2,0:T(8,128)(2,1)}, u32[]{:S(2)}) copy-start(bf16[2,256,1024]{1,2,0:T(8,128)(2,1)} %copy-done.17) | copy-start | bytes 3145732
  217.2 2.8 copy-start.10
  221.6 7.5 %copy-start.14 = (bf16[16,2,8,1024]{3,2,1,0:T(8,128)(2,1)S(1)}, bf16[16,2,8,1024]{3,2,1,0:T(8,128)(2,1)}, u32[]{:S(2)}) copy-start(bf16[16,2,8,1024]{3,2,1,0:T(8,128)(2,1)} %copy-done.13) | copy-start | bytes 1572868
  231.2 5.4 %copy-start.39 = (bf16[2,128,2048]{2,1,0:T(8,128)(2,1)}, bf16[2,128,2048]{2,1,0:T(8,128)(2,1)S(1)}, u32[]{:S(2)}) copy-start(bf16[2,128,2048]{2,1,0:T(8,128)(2,1)S(1)} %fusion.39) | copy-start | bytes 3145732
  238.2 3.8 copy-start.33
  238.2 3.8 copy-start.35
  238.2 3.8 copy-start.38
  239.9 5.2 %copy-start.40 = (bf16[2,128,2048]{2,1,0:T(8,128)(2,1)S(1)}, bf16[2,128,2048]{2,1,0:T(8,128)(2,1)}, u32[]{:S(2)}) copy-start(bf16[2,128,2048]{2,1,0:T(8,128)(2,1)} %copy-done.39) | copy-start | bytes 3145732
  373.6 2.9 copy-start.53
  392.8 28.4 %copy-start.1 = (bf16[1024,1024]{1,0:T(8,128)(2,1)S(1)}, bf16[1024,1024]{1,0:T(8,128)(2,1)}, u32[]{:S(2)}) copy-start(bf16[1024,1024]{1,0:T(8,128)(2,1)} %param.42) | copy-start | bytes 6291460
  (28 other events, 38.5 us)
Sparse Core Ops, SparseCore 0:
  242.1 174.4 all-reduce.3

commit v2 on v1

v2 whole, which is shorter than its diff:
```python
import functools
from types import SimpleNamespace as Names

import jax
import jax.numpy as jnp
from jax import lax
from jax.experimental import pallas as pl
from jax.experimental.pallas import tpu as pltpu
from jax.sharding import PartitionSpec as P

HEAD_DIM = 64
EPSILON = 1e-05
MASKED_SCORE = -1e30
MESH = pl.DeviceIdType.MESH
ANY = pl.BlockSpec(memory_space=pl.ANY)
VMEM = pl.BlockSpec(memory_space=pltpu.VMEM)
SMEM = pl.BlockSpec(memory_space=pltpu.SMEM)
LANES = 128
F32, BF16 = jnp.float32, jnp.bfloat16
ROWS, WIDTH, HIDDEN = 256, 1024, 4096
PAIRS = WIDTH // LANES
HIDE = 512

SP_KEY, SP_VALUE, SP_QUERY, SP_ROWS = 1024, 1536, 2048, 2304
TP_KEY, TP_VALUE, TP_QUERY, TP_ROWS = 512, 768, 1024, 1280

ORDERS = (("x", "y", "z"), ("y", "z", "x"), ("z", "x", "y"))
MATRICES = (
    (HIDDEN, WIDTH, (1, 1, 2)),
    (WIDTH, HIDDEN, (6, 6, 4)),
    (WIDTH, WIDTH, (1, 2, 1)),
    (WIDTH, 3 * WIDTH, (4, 4, 4)),
    (WIDTH, WIDTH, (2, 1, 1)),
    (WIDTH, 3 * WIDTH, (4, 4, 4)),
)
SEND_UNITS = (0, 16, 12, 0, 28, 16)


class Place:
    def __init__(self):
        ta, col = lax.axis_index("ta"), lax.axis_index("col")
        self.ta, self.col = ta, col
        self.y_hi, self.x, self.core = ta // 8, (ta // 2) % 4, ta % 2
        self.y_lo, self.z = col // 4, col % 4
        self.y = self.y_hi * 2 + self.y_lo
        self.partner = self.device(core=1 - self.core)

    def device(self, y_hi=None, x=None, core=None, y_lo=None, z=None):
        y_hi = self.y_hi if y_hi is None else y_hi
        x = self.x if x is None else x
        core = self.core if core is None else core
        y_lo = self.y_lo if y_lo is None else y_lo
        z = self.z if z is None else z
        return (y_hi * 8 + x * 2 + core, y_lo * 4 + z)

    def along(self, axis, step):
        if axis == "x":
            at = (self.x + step) % 4
            return self.device(x=at), at
        if axis == "z":
            at = (self.z + step) % 4
            return self.device(z=at), at
        at = (self.y + step) % 4
        return self.device(y_hi=at // 2, y_lo=at % 2), (at % 2) * 2 + at // 2

    def fellow(self, step):
        ta = (self.ta + step) % 16
        return (ta, self.col), ta


def greet(place, whole):
    barrier = pltpu.get_barrier_semaphore()

    def one(step, carry):
        pl.semaphore_signal(barrier, inc=1, device_id=place.fellow(step)[0], device_id_type=MESH)
        return carry

    lax.fori_loop(1, 16, one, 0)
    count = 15
    if whole:
        for axis, step in (("y", 1), ("y", 3), ("z", 1), ("z", 2), ("z", 3)):
            pl.semaphore_signal(barrier, inc=1, device_id=place.along(axis, step)[0], device_id_type=MESH)
            count += 1
    pl.semaphore_wait(barrier, count)


def remote(source, target, send, recv, device):
    return pltpu.make_async_remote_copy(source, target, send, recv, device_id=device, device_id_type=MESH)


def dot(left, right):
    return jnp.dot(left, right, preferred_element_type=F32)


def dot_nt(left, right):
    return lax.dot_general(left, right, (((1,), (1,)), ((), ())), preferred_element_type=F32)


def dot_tn(left, right):
    return lax.dot_general(left, right, (((0,), (0,)), ((), ())), preferred_element_type=F32)


def rows16(step):
    return pl.ds(pl.multiple_of(step * 16, 16), 16)


def lanes(step, width):
    return pl.ds(pl.multiple_of(step * width, width), width)


def interleave(big, small):
    width = big.shape[-1]
    pair = [one.reshape(-1, 1, 8, width) for one in (big, small)]
    return jnp.concatenate(pair, axis=1).reshape(-1, width)


def family(rows, which):
    width = rows.shape[-1]
    return rows.reshape(-1, 2, 8, width)[:, which].reshape(-1, width)


def half_masks(rows):
    lane = lax.broadcasted_iota(jnp.int32, (rows, LANES), 1)
    return lane < HEAD_DIM


def by_head(value, low):
    zero = jnp.zeros_like(value)
    return jnp.where(low, value, zero), jnp.where(low, zero, value)


def statistics(rows):
    mean = jnp.mean(rows, axis=-1, keepdims=True)
    centered = rows - mean
    variance = jnp.mean(centered * centered, axis=-1, keepdims=True)
    scale = lax.rsqrt(variance + EPSILON)
    return centered * scale, scale


def norm_forward(source, gain, shift, target, normals, scales, after=None):
    def one(step, carry):
        rows = rows16(step)
        normal, scale = statistics(source[rows])
        target[rows] = (normal * gain + shift).astype(BF16)
        normals[rows] = normal
        scales[rows] = jnp.broadcast_to(scale, (16, LANES))
        if after is not None:
            after(step)
        return carry

    lax.fori_loop(0, 16, one, 0, unroll=2)


def transpose_into(source, target):
    def one(step, carry):
        target[step] = source[:, lanes(step, LANES)].T
        return carry

    lax.fori_loop(0, PAIRS, one, 0)


class Swap:
    def __init__(self, place, send, recv, sems, index, to_positions, columns=slice(0, WIDTH)):
        self.place, self.send, self.recv, self.sems, self.index = place, send, recv, sems, index
        self.to_positions, self.columns = to_positions, columns

    def rows(self, ta):
        frames = rows16(ta)
        positions = rows16((ta % 2) * 8 + ta // 2)
        return (frames, positions) if self.to_positions else (positions, frames)

    def copy(self, step):
        device, ta = self.place.fellow(step)
        source = self.send.at[self.rows(ta)[0], self.columns]
        target = self.recv.at[self.rows(self.place.ta)[1], self.columns]
        return remote(source, target, self.sems.at[self.index, 0, step], self.sems.at[self.index, 1, step], device)

    def own(self):
        rows = self.rows(self.place.ta)
        source, target = self.send.at[rows[0], self.columns], self.recv.at[rows[1], self.columns]
        return pltpu.make_async_copy(source, target, self.sems.at[self.index, 0, 0])

    def start_block(self, ta):
        step = (ta - self.place.ta + 16) % 16

        @pl.when(step > 0)
        def _():
            self.copy(step).start()

        @pl.when(step == 0)
        def _():
            self.own().start()

    def start(self):
        def one(step, carry):
            self.copy(step).start()
            return carry

        lax.fori_loop(1, 16, one, 0)
        self.own().start()

    def wait(self):
        def one(step, carry):
            self.copy(step).wait_recv()
            return carry

        self.own().wait()
        lax.fori_loop(1, 16, one, 0)

    def sent(self):
        def one(step, carry):
            self.copy(step).wait_send()
            return carry

        lax.fori_loop(1, 16, one, 0)


HALVES = (slice(0, WIDTH // 2), slice(WIDTH // 2, WIDTH))


FORWARD_OUTS = dict(
    big_out=((128, WIDTH), BF16),
    small_out=((128, WIDTH), BF16),
    normal1=((ROWS, WIDTH), F32),
    normal2=((ROWS, WIDTH), F32),
    normal3=((ROWS, WIDTH), F32),
    scale1=((ROWS, LANES), F32),
    scale2=((ROWS, LANES), F32),
    scale3=((ROWS, LANES), F32),
    normed1_t=((PAIRS, LANES, ROWS), BF16),
    context1_t=((PAIRS, LANES, ROWS), BF16),
    normed2_t=((PAIRS, LANES, ROWS), BF16),
    context2_t=((PAIRS, LANES, ROWS), BF16),
    normed3_t=((PAIRS, LANES, ROWS), BF16),
    activated_t=((PAIRS, HIDE, ROWS), BF16),
    spatial=((PAIRS, SP_ROWS, LANES), BF16),
    temporal=((PAIRS, TP_ROWS, LANES), BF16),
    slope=((PAIRS, ROWS, HIDE), BF16),
)
FORWARD_WORK = dict(
    w_sqkv=((WIDTH, 3 * WIDTH), BF16),
    w_sout=((WIDTH, WIDTH), BF16),
    w_tqkv=((WIDTH, 3 * WIDTH), BF16),
    w_tout=((WIDTH, WIDTH), BF16),
    w_fin=((WIDTH, HIDDEN), BF16),
    w_fout=((HIDDEN, WIDTH), BF16),
    normed=((ROWS, WIDTH), BF16),
    context=((ROWS, WIDTH), BF16),
    arranged=((ROWS, WIDTH), BF16),
    context_send=((ROWS, WIDTH), BF16),
    context_back=((ROWS, WIDTH), BF16),
    normed3=((ROWS, WIDTH), BF16),
    total=((ROWS, WIDTH), F32),
    hidden=((ROWS, HIDE), F32),
    params=((16, WIDTH), F32),
    inner_bias=((PAIRS, HIDE), F32),
    table=((8, WIDTH), F32),
)


def named(keys, refs):
    return Names(**{key: refs.pop(0) for key in keys})


def forward_kernel(in_keys, vector_count, weight_keys, *refs):
    refs = list(refs)
    ins = named(in_keys, refs)
    vectors = [refs.pop(0) for _ in range(vector_count)]
    weights = named(weight_keys, refs)
    outs, keep, work = named(FORWARD_OUTS, refs), named(FORWARD_OUTS, refs), named(FORWARD_WORK, refs)
    w_sems, out_sems, swap_sems, far_sems = refs
    place = Place()
    params = work.params

    def param(row):
        return params[row : row + 1]

    loads = Names()
    for i, key in enumerate(weight_keys):
        setattr(loads, key, pltpu.make_async_copy(getattr(weights, key), getattr(work, key), w_sems.at[i]))
    loads.w_sqkv.start()
    for row, vector in enumerate(vectors):
        params[row : row + 1] = vector[...].astype(F32).reshape(1, WIDTH)
    for row in range(PAIRS):
        at = slice(row * HIDE, row * HIDE + HIDE)
        work.inner_bias[row : row + 1] = ins.inner_bias[at].astype(F32).reshape(1, HIDE)
    work.table[...] = ins.table[...].astype(F32)
    frame = place.ta // 2
    copies = []

    def save(source, target):
        copy = pltpu.make_async_copy(source, target, out_sems.at[len(copies)])
        copy.start()
        copies.append(copy)

    resid0, resid1, resid2 = keep.normal2, keep.normal3, work.total
    big_row = work.table[pl.ds(ins.big_actions[0, frame], 1)]

    def start_rows(step, carry):
        near = pl.ds(pl.multiple_of(step * 16, 16), 16)
        big = ins.big[near].astype(F32) + big_row
        small = ins.small[near].astype(F32) + work.table[pl.ds(ins.small_actions[step // 2, frame], 1)]
        rows = pl.ds(pl.multiple_of(step * 32, 32), 32)
        merged = interleave(big, small)
        resid0[rows] = merged
        normal, scale = statistics(merged)
        work.normed[rows] = (normal * param(0) + param(1)).astype(BF16)
        keep.normal1[rows] = normal
        keep.scale1[rows] = jnp.broadcast_to(scale, (32, LANES))
        return carry

    lax.fori_loop(0, 8, start_rows, 0)
    save(keep.normal1, outs.normal1)
    save(keep.scale1, outs.scale1)
    greet(place, False)

    spatial = keep.spatial
    loads.w_sqkv.wait()
    for key in weight_keys[1:]:
        getattr(loads, key).start()

    def spatial_project(column, base, per_family, scale):
        def one(step, carry):
            at = column + step
            value = dot(work.normed[...], work.w_sqkv[:, lanes(at, 256)]) * scale
            for which in range(2):
                one_family = family(value, which).astype(BF16)
                rows = pl.ds(base + which * per_family, 128)
                spatial[step * 2, rows] = one_family[:, :LANES]
                spatial[step * 2 + 1, rows] = one_family[:, LANES:]
            return carry

        lax.fori_loop(0, 4, one, 0)

    spatial_project(4, SP_KEY, 256, 1.0)
    spatial_project(8, SP_VALUE, 256, 1.0)
    far = []
    for i, base in enumerate((SP_KEY, SP_KEY + 256, SP_VALUE, SP_VALUE + 256)):
        far.append(
            remote(
                spatial.at[:, pl.ds(base, 128)], spatial.at[:, pl.ds(base + 128, 128)],
                far_sems.at[0, i], far_sems.at[1, i], place.partner,
            )
        )
    for copy in far:
        copy.start()
    spatial_project(0, SP_QUERY, 128, 0.125)
    transpose_into(work.normed, keep.normed1_t)
    save(keep.normed1_t, outs.normed1_t)
    for copy in far:
        copy.wait()

    low_q, low_k = half_masks(128), half_masks(256)
    key_slot = (lax.broadcasted_iota(jnp.int32, (256, 128), 0) % 128) // 32
    query_slot = lax.broadcasted_iota(jnp.int32, (256, 128), 1) // 32
    same_slot = key_slot == query_slot

    def softmax(scores):
        weights_ = jnp.exp(scores - jnp.max(scores, axis=0, keepdims=True))
        return (weights_ * (1.0 / jnp.sum(weights_, axis=0, keepdims=True))).astype(BF16)

    def spatial_pair(pair, carry):
        contexts = []
        for which in range(2):
            keys = spatial[pair, SP_KEY + which * 256 : SP_KEY + which * 256 + 256]
            values = spatial[pair, SP_VALUE + which * 256 : SP_VALUE + which * 256 + 256]
            queries = by_head(spatial[pair, SP_QUERY + which * 128 : SP_QUERY + which * 128 + 128], low_q)
            probs = []
            for head in range(2):
                scores = dot_nt(keys, queries[head])
                if which == 1:
                    scores = jnp.where(same_slot, scores, MASKED_SCORE)
                prob = softmax(scores)
                at = (which * 2 + head) * 256
                spatial[pair, at : at + 256] = prob
                probs.append(prob)
            contexts.append(
                dot_tn(jnp.concatenate(probs, axis=0), jnp.concatenate(by_head(values, low_k), axis=0))
            )
        work.context[:, lanes(pair, LANES)] = interleave(*contexts).astype(BF16)
        return carry

    lax.fori_loop(0, PAIRS, spatial_pair, 0)
    save(keep.spatial, outs.spatial)

    def project_into(source, weight, bias, before, target):
        def one(step, carry):
            at = lanes(step, 256)
            target[:, at] = dot(source[...], weight[:, at]) + params[bias : bias + 1, at] + before[:, at]
            return carry

        lax.fori_loop(0, WIDTH // 256, one, 0)

    loads.w_sout.wait()
    project_into(work.context, work.w_sout, 2, resid0, resid1)
    there = Swap(place, work.normed, work.arranged, swap_sems, 0, True)
    norm_forward(resid1, param(3), param(4), work.normed, keep.normal2, keep.scale2, there.start_block)
    save(keep.normal2, outs.normal2)
    save(keep.scale2, outs.scale2)
    transpose_into(work.context, keep.context1_t)
    save(keep.context1_t, outs.context1_t)
    loads.w_tqkv.wait()
    there.wait()

    temporal = keep.temporal

    def temporal_project(column, base, scale):
        def one(step, carry):
            value = dot(work.arranged[...], work.w_tqkv[:, lanes(column + step, 256)]) * scale
            value = value.astype(BF16)
            temporal[step * 2, base : base + ROWS] = value[:, :LANES]
            temporal[step * 2 + 1, base : base + ROWS] = value[:, LANES:]
            return carry

        lax.fori_loop(0, 4, one, 0)

    temporal_project(0, TP_QUERY, 0.125)
    temporal_project(4, TP_KEY, 1.0)
    temporal_project(8, TP_VALUE, 1.0)
    key_row = lax.broadcasted_iota(jnp.int32, (128, 128), 0)
    query_row = lax.broadcasted_iota(jnp.int32, (128, 128), 1)
    key_rank, query_rank = jnp.zeros_like(key_row), jnp.zeros_like(query_row)
    for at in range(8):
        big_rank, small_rank = ins.big_order[0, at], ins.small_order[place.ta // 4, at]
        key_rank = jnp.where(key_row // 16 == at, jnp.where(key_row % 16 < 8, big_rank, small_rank), key_rank)
        query_rank = jnp.where(query_row // 16 == at, jnp.where(query_row % 16 < 8, big_rank, small_rank), query_rank)
    seen = (key_row % 16 == query_row % 16) & (key_rank <= query_rank)

    def temporal_pair(pair, carry):
        contexts = []
        for half in range(2):
            keys = temporal[pair, TP_KEY + half * 128 : TP_KEY + half * 128 + 128]
            values = temporal[pair, TP_VALUE + half * 128 : TP_VALUE + half * 128 + 128]
            queries = by_head(temporal[pair, TP_QUERY + half * 128 : TP_QUERY + half * 128 + 128], low_q)
            probs = []
            for head in range(2):
                prob = softmax(jnp.where(seen, dot_nt(keys, queries[head]), MASKED_SCORE))
                at = (half * 2 + head) * 128
                temporal[pair, at : at + 128] = prob
                probs.append(prob)
            contexts.append(
                dot_tn(jnp.concatenate(probs, axis=0), jnp.concatenate(by_head(values, low_q), axis=0))
            )
        work.context_send[:, lanes(pair, LANES)] = jnp.concatenate(contexts, axis=0).astype(BF16)
        return carry

    back = [Swap(place, work.context_send, work.context_back, swap_sems, 1 + i, False, HALVES[i]) for i in range(2)]
    lax.fori_loop(0, PAIRS // 2, temporal_pair, 0)
    back[0].start()
    lax.fori_loop(PAIRS // 2, PAIRS, temporal_pair, 0)
    back[1].start()
    save(keep.temporal, outs.temporal)
    transpose_into(work.arranged, keep.normed2_t)
    save(keep.normed2_t, outs.normed2_t)
    loads.w_tout.wait()
    for i in range(2):
        back[i].wait()

        def add_half(step, carry, i=i):
            at = lanes(step, 256)
            value = dot(work.context_back[:, HALVES[i]], work.w_tout[HALVES[i], at])
            if i == 0:
                resid2[:, at] = value + params[5:6, at] + resid1[:, at]
            else:
                resid2[:, at] += value
            return carry

        lax.fori_loop(0, WIDTH // 256, add_half, 0)
    norm_forward(resid2, param(6), param(7), work.normed3, keep.normal3, keep.scale3)
    save(keep.normal3, outs.normal3)
    save(keep.scale3, outs.scale3)
    transpose_into(work.context_back, keep.context2_t)
    save(keep.context2_t, outs.context2_t)
    transpose_into(work.normed3, keep.normed3_t)
    save(keep.normed3_t, outs.normed3_t)

    total, hidden, slope = work.total, work.hidden, keep.slope
    total[...] += param(8)
    loads.w_fin.wait()
    loads.w_fout.wait()
    root = 0.7978845608028654

    def feed(step, carry):
        hidden[...] = dot(work.normed3[...], work.w_fin[:, lanes(step, HIDE)])

        def some(part, inner):
            rows = pl.ds(pl.multiple_of(part * 32, 32), 32)
            value = hidden[rows] + work.inner_bias[pl.ds(step, 1)]
            square = value * value
            bent = jnp.tanh(root * value * (1.0 + 0.044715 * square))
            half = 0.5 * (1.0 + bent)
            work.context_send[rows, :HIDE] = (value * half).astype(BF16)
            rise = half + 0.5 * value * (1.0 - bent * bent) * (root * (1.0 + 0.134145 * square))
            slope[step, rows] = rise.astype(BF16)
            return inner

        lax.fori_loop(0, 8, some, 0)
        active = work.context_send[:, :HIDE]
        for block in range(HIDE // LANES):
            at = slice(block * LANES, block * LANES + LANES)
            keep.activated_t[step, at] = work.context_send[:, at].T
        down = work.w_fout.at[pl.ds(pl.multiple_of(step * HIDE, HIDE), HIDE)]
        for column in range(WIDTH // 256):
            at = slice(column * 256, column * 256 + 256)
            total[:, at] += dot(active, down[:, at])
        return carry

    for one in back:
        one.sent()
    lax.fori_loop(0, PAIRS, feed, 0)
    save(keep.slope, outs.slope)
    save(keep.activated_t, outs.activated_t)

    def finish_rows(step, carry):
        value = total[pl.ds(pl.multiple_of(step * 32, 32), 32)]
        near = pl.ds(pl.multiple_of(step * 16, 16), 16)
        keep.big_out[near] = family(value, 0).astype(BF16)
        keep.small_out[near] = (family(value, 1) * ins.live[step // 2].astype(F32)).astype(BF16)
        return carry

    lax.fori_loop(0, 8, finish_rows, 0)
    save(keep.big_out, outs.big_out)
    save(keep.small_out, outs.small_out)
    there.sent()
    for copy in copies:
        copy.wait()


def forward(ins, scalars, vectors, weights):
    sem = pltpu.SemaphoreType.DMA
    kept, work = list(FORWARD_OUTS.values()), list(FORWARD_WORK.values())
    in_keys, weight_keys = tuple(vars(ins)) + tuple(vars(scalars)), tuple(vars(weights))
    results = pl.pallas_call(
        functools.partial(forward_kernel, in_keys, len(vectors), weight_keys),
        out_shape=[jax.ShapeDtypeStruct(shape, dtype) for shape, dtype in kept],
        in_specs=[VMEM] * len(vars(ins)) + [SMEM] * len(vars(scalars)) + [VMEM] * len(vectors) + [ANY] * len(weight_keys),
        out_specs=[ANY] * len(kept),
        scratch_shapes=[pltpu.VMEM(shape, dtype) for shape, dtype in kept + work]
        + [sem((len(weight_keys),)), sem((len(kept),)), sem((3, 2, 16)), sem((2, 4))],
        compiler_params=pltpu.CompilerParams(
            collective_id=1, has_side_effects=True, vmem_limit_bytes=62 * 2**20
        ),
        cost_estimate=pl.CostEstimate(flops=9 * 10**9, bytes_accessed=60 * 2**20, transcendentals=4 * 10**6),
        name="layer_forward",
    )(*vars(ins).values(), *vars(scalars).values(), *vectors, *vars(weights).values())
    return named(FORWARD_OUTS, list(results))


class Reduction:
    def __init__(self, place, index, refs, sems):
        self.place, self.index, self.refs, self.sems = place, index, refs, sems
        k, n, shares = MATRICES[index]
        self.half = n // 2
        self.depth = k // 64
        self.groups = self.depth // 16
        self.bounds, start = [], 0
        for share in shares:
            self.bounds.append((start, start + share))
            start += share
        self.units = start * self.groups
        self.first_unit = sum(m[1] // 2 // LANES * (m[0] // 1024) for m in MATRICES[:index])
        self.send_unit = SEND_UNITS[index]
        self.local_done = False

    def left_local(self):
        r, s, i = self.refs, self.sems, self.index
        return pltpu.make_async_copy(r.at_in, r.at.at[:, :, :, :, :, :ROWS], s.local.at[i, 0])

    def left_far(self):
        r, s, i = self.refs, self.sems, self.index
        target = r.at.at[:, :, :, :, :, ROWS:]
        return remote(r.at_in, target, s.ex_send.at[i, 0], s.ex_recv.at[i, 0], self.place.partner)

    def right_local(self):
        r, s, i, core = self.refs, self.sems, self.index, self.place.core
        source = r.source.at[:, lanes(core, self.half)]
        return pltpu.make_async_copy(source, r.g.at[:ROWS], s.local.at[i, 1])

    def right_far(self):
        r, s, i, core = self.refs, self.sems, self.index, self.place.core
        source = r.source.at[:, lanes(1 - core, self.half)]
        return remote(source, r.g.at[ROWS:], s.ex_send.at[i, 1], s.ex_recv.at[i, 1], self.place.partner)

    def lefts(self):
        self.left_far().start()
        self.left_local().start()

    def rights(self):
        self.right_far().start()
        self.right_local().start()

    def right_local_done(self):
        if not self.local_done:
            self.right_local().wait()
            self.local_done = True

    def rights_sent(self):
        self.right_local_done()
        self.right_far().wait_send()

    def loaded(self):
        self.left_far().wait_recv()
        self.right_far().wait_recv()
        self.left_local().wait()
        self.right_local_done()

    def span(self, part):
        low, high = self.bounds[part]
        return low * self.groups, high * self.groups

    def copy(self, part, stage, step):
        r, s, i = self.refs, self.sems, self.index
        low, high = self.span(part)
        here = slice(self.first_unit + low, self.first_unit + high)
        device, slot = self.place.along(ORDERS[part][stage], step)
        if stage == 1:
            source = r.r1.at[0, here, slot]
            target = r.r2.at[step - 1, here]
        else:
            source = r.r2.at[0, here, slot]
            target = r.r3.at[step - 1, here]
        return remote(
            source, target, s.send.at[i, part, stage, step - 1], s.recv.at[i, part, stage, step - 1], device
        )

    def left_block(self, part, slot, group):
        at = self.refs.at
        rows = slice(group * 16, group * 16 + 16)
        if part == 0:
            blocks = [at[y // 2, :, y % 2, slot, rows] for y in range(4)]
        elif part == 1:
            blocks = [at[slot // 2, :, slot % 2, :, rows]]
        else:
            blocks = [at[:, slot, :, x, rows] for x in range(4)]
        blocks = [block.reshape(-1, block.shape[-1]) for block in blocks]
        return blocks[0] if len(blocks) == 1 else jnp.concatenate(blocks, axis=0)

    def products(self, part, slot, emit):
        low, high = self.bounds[part]
        for group in range(self.groups):
            left = self.left_block(part, slot, group)
            for tile in range(low, high, 2):
                width = min(2, high - tile)
                value = dot(left, self.refs.g[:, tile * LANES : (tile + width) * LANES])
                for i in range(width):
                    one = value[:, i * LANES : (i + 1) * LANES].reshape(4, 4, 16, LANES)
                    emit((tile + i) * self.groups + group, one)

    def relay(self, part, way):
        r, s, i = self.refs, self.sems, self.index
        low, high = self.span(part)
        here = slice(self.first_unit + low, self.first_unit + high)
        half = slice(way * 2, way * 2 + 2)
        device = self.place.along(ORDERS[part][0], 3 if way else 1)[0]
        source = r.s1.at[0, self.send_unit + low : self.send_unit + high, half]
        target = r.r1.at[2, here, half]
        return remote(source, target, s.send.at[i, part, 0, way], s.recv.at[i, part, 0, way], device)

    def direct(self, part, way):
        r, s, i = self.refs, self.sems, self.index
        low, high = self.span(part)
        here = slice(self.first_unit + low, self.first_unit + high)
        device = self.place.along(ORDERS[part][0], 3 if way else 1)[0]
        source = r.s1.at[1 + way, self.send_unit + low : self.send_unit + high]
        target = r.r1.at[way, here]
        return remote(source, target, s.send.at[i, part, 0, 2 + way], s.recv.at[i, part, 0, 2 + way], device)

    def first(self):
        r = self.refs
        for part in range(3):
            slot = self.place.along(ORDERS[part][0], 2)[1]

            def emit(unit, value):
                r.s1[0, self.send_unit + unit] = value.astype(BF16)

            self.products(part, slot, emit)
            for way in range(2):
                self.relay(part, way).start()

    def pass_on(self):
        r = self.refs
        for part in range(3):
            for way in range(2):
                self.relay(part, way).wait_recv()
                slot = self.place.along(ORDERS[part][0], 3 if way else 1)[1]

                def emit(unit, value, way=way):
                    at = self.first_unit + unit
                    for half in range(2):
                        some = slice(half * 2, half * 2 + 2)
                        one = value[some]
                        if half == way:
                            one = one + r.r1[2, at, some].astype(F32)
                        r.s1[1 + way, self.send_unit + unit, some] = one.astype(BF16)

                self.products(part, slot, emit)
                self.direct(part, way).start()

    def first_sent(self):
        for part in range(3):
            for way in range(2):
                self.relay(part, way).wait_send()
                self.direct(part, way).wait_send()

    def second(self):
        r = self.refs
        for part in range(3):
            slot = self.place.along(ORDERS[part][0], 0)[1]
            for way in range(2):
                self.direct(part, way).wait_recv()

            def emit(unit, value):
                at = self.first_unit + unit
                for i in range(2):
                    value = value + r.r1[i, at].astype(F32)
                r.r1[0, at] = value.astype(BF16)

            self.products(part, slot, emit)
            for step in (1, 2, 3):
                self.copy(part, 1, step).start()

    def third(self):
        r = self.refs
        for part in range(3):
            slot = self.place.along(ORDERS[part][1], 0)[1]
            for step in (1, 2, 3):
                self.copy(part, 1, step).wait_recv()

            def one(unit, carry, slot=slot):
                value = r.r1[0, unit, slot].astype(F32)
                for i in range(3):
                    value = value + r.r2[i, unit].astype(F32)
                r.r2[0, unit] = value.astype(BF16)
                return carry

            low, high = self.span(part)
            lax.fori_loop(self.first_unit + low, self.first_unit + high, one, 0)
            for step in (1, 2, 3):
                self.copy(part, 2, step).start()

    def mine(self):
        return self.place.y_hi * 4 + self.place.x

    def rows_of(self, slot):
        return pl.ds(pl.multiple_of(slot * self.depth, self.depth), self.depth)

    def gather_copy(self, y_hi, x, slot):
        r, s, i, place = self.refs, self.sems, self.index, self.place
        target = r.out.at[self.rows_of(slot), lanes(place.core, self.half)]
        return remote(
            r.piece, target, s.ag_send.at[i, y_hi * 4 + x], s.ag_recv.at[i, slot],
            place.device(y_hi=y_hi, x=x),
        )

    def own_copy(self):
        target = self.refs.out.at[self.rows_of(self.mine()), lanes(self.place.core, self.half)]
        return pltpu.make_async_copy(self.refs.piece, target, self.sems.local.at[self.index, 2])

    def others(self):
        place = self.place
        for y_step in (0, 1):
            y_hi = (place.y_hi + y_step) % 2
            for x_step in range(4):
                if y_step or x_step:
                    yield y_hi, (place.x + x_step) % 4

    def fourth(self):
        r = self.refs
        for part in range(3):
            slot = self.place.along(ORDERS[part][2], 0)[1]
            for step in (1, 2, 3):
                self.copy(part, 2, step).wait_recv()
            low, high = self.span(part)
            for unit in range(low, high):
                at = self.first_unit + unit
                value = r.r2[0, at, slot].astype(F32)
                for i in range(3):
                    value = value + r.r3[i, at].astype(F32)
                tile, group = unit // self.groups, unit % self.groups
                r.piece[group * 16 : group * 16 + 16, tile * LANES : tile * LANES + LANES] = value.astype(BF16)
        self.own_copy().start()
        for y_hi, x in self.others():
            self.gather_copy(y_hi, x, self.mine()).start()

    def cross_copy(self):
        r, s, i, core = self.refs, self.sems, self.index, self.place.core
        block = r.out.at[:, lanes(core, self.half)]
        return remote(block, block, s.cross.at[i, 0], s.cross.at[i, 1], self.place.partner)

    def fifth(self):
        self.own_copy().wait()
        for y_hi, x in self.others():
            self.gather_copy(y_hi, x, y_hi * 4 + x).wait_recv()
        self.cross_copy().start()

    def finish(self):
        self.cross_copy().wait()
        self.left_far().wait_send()
        for y_hi, x in self.others():
            self.gather_copy(y_hi, x, self.mine()).wait_send()
        for part in range(3):
            for stage in (1, 2):
                for step in (1, 2, 3):
                    self.copy(part, stage, step).wait_send()


GAIN1, SHIFT1, SPATIAL_BIAS, GAIN2, SHIFT2, TEMPORAL_BIAS, GAIN3, SHIFT3, INNER, OUTER = 8, 9, 10, 11, 12, 13, 14, 15, 16, 20


class SmallSums:
    def __init__(self, place, refs, sems):
        self.place, self.refs, self.sems = place, refs, sems

    def share(self, core):
        return pl.ds(pl.multiple_of(core * 16, 16), 16)

    def cross(self):
        r, core = self.refs, self.place.core
        return remote(
            r.sums.at[self.share(1 - core)], r.sums_core, self.sems.at[0, 0, 0], self.sems.at[1, 0, 0],
            self.place.partner,
        )

    def along(self, stage, step):
        device = self.place.along("xyz"[stage], step)[0]
        return remote(
            self.refs.sums_total.at[stage], self.refs.sums_recv.at[stage, step - 1],
            self.sems.at[0, stage + 1, step - 1], self.sems.at[1, stage + 1, step - 1], device,
        )

    def final(self):
        block = self.refs.sums_final.at[self.share(self.place.core)]
        return remote(block, block, self.sems.at[0, 4, 0], self.sems.at[1, 4, 0], self.place.partner)

    def begin(self):
        self.cross().start()

    def step0(self):
        r = self.refs
        self.cross().wait()
        r.sums_total[0] = r.sums[self.share(self.place.core)] + r.sums_core[...]
        for step in (1, 2, 3):
            self.along(0, step).start()

    def advance(self, stage):
        r = self.refs
        value = r.sums_total[stage]
        for step in (1, 2, 3):
            self.along(stage, step).wait_recv()
            value = value + r.sums_recv[stage, step - 1]
        if stage < 2:
            r.sums_total[stage + 1] = value
            for step in (1, 2, 3):
                self.along(stage + 1, step).start()
        else:
            r.sums_final[self.share(self.place.core)] = value
            self.final().start()

    def finish(self, out, sem):
        self.final().wait()
        copy = pltpu.make_async_copy(self.refs.sums_final, out, sem)
        copy.start()
        for stage in range(3):
            for step in (1, 2, 3):
                self.along(stage, step).wait_send()
        copy.wait()


BACK_OUTS = dict(
    big_grad=((128, WIDTH), F32),
    small_grad=((128, WIDTH), F32),
    small_sums=((32, WIDTH), F32),
)
SLOTS = 3
BACK_WORK = dict(
    s1=((3, 32, 4, 4, 16, LANES), BF16),
    r1=((3, 64, 4, 4, 16, LANES), BF16),
    r2=((3, 64, 4, 16, LANES), BF16),
    r3=((3, 64, 16, LANES), BF16),
    tall=((SLOTS, HIDE, WIDTH), BF16),
    broad=((SLOTS, WIDTH, HIDE), BF16),
    slope_in=((SLOTS, ROWS, HIDE), BF16),
    record=((SLOTS, SP_ROWS, LANES), BF16),
    resid=((ROWS, WIDTH), F32),
    grad=((ROWS, WIDTH), F32),
    total=((ROWS, WIDTH), F32),
    low3=((ROWS, WIDTH), BF16),
    low2=((ROWS, WIDTH), BF16),
    low1=((ROWS, WIDTH), BF16),
    hidden_low=((ROWS, HIDDEN), BF16),
    packed=((ROWS, 3 * WIDTH), BF16),
    swap_send=((ROWS, WIDTH), BF16),
    context_back=((ROWS, WIDTH), BF16),
    normed_back=((ROWS, WIDTH), BF16),
    context_grad=((2, 128, WIDTH), BF16),
    far_send=((ROWS, 2 * WIDTH), BF16),
    far_recv=((ROWS, 2 * WIDTH), BF16),
    inner_sums=((PAIRS, HIDE), F32),
    sums=((32, WIDTH), F32),
    sums_core=((16, WIDTH), F32),
    sums_total=((3, 16, WIDTH), F32),
    sums_recv=((3, 3, 16, WIDTH), F32),
    sums_final=((32, WIDTH), F32),
    frame_sums=((8, WIDTH), F32),
    scale=((ROWS, LANES), F32),
    gains=((8, WIDTH), F32),
)


BACK_SEMS = dict(
    local=(6, 3),
    ex_send=(6, 2),
    ex_recv=(6, 2),
    send=(6, 3, 3, 4),
    recv=(6, 3, 3, 4),
    ag_send=(6, 8),
    ag_recv=(6, 8),
    cross=(6, 2),
    ring=(4, SLOTS),
    io=(5,),
    swap=(3, 2, 16),
    far=(2,),
    sums=(2, 5, 3),
)


def backward_kernel(in_keys, saved_keys, weight_keys, *refs):
    refs = list(refs)
    count = len(MATRICES)
    ins = named(in_keys, refs)
    gains = [refs.pop(0) for _ in range(3)]
    lefts = [refs.pop(0) for _ in range(count)]
    saved, weights, outs = named(saved_keys, refs), named(weight_keys, refs), named(BACK_OUTS, refs)
    matrix_outs = [refs.pop(0) for _ in range(count)]
    work = named(BACK_WORK, refs)
    ats, gs, pieces = ([refs.pop(0) for _ in range(count)] for _ in range(3))
    sems = named(BACK_SEMS, refs)
    ring_sems, io_sems, swap_sems, far_sems, sum_sems = sems.ring, sems.io, sems.swap, sems.far, sems.sums
    place = Place()
    frame = place.ta // 2
    sources = (work.low3, work.hidden_low, work.low2, work.packed, work.low1, work.packed)
    reductions = []
    for i in range(count):
        own = Names(at_in=lefts[i], at=ats[i], g=gs[i], piece=pieces[i], out=matrix_outs[i], source=sources[i])
        own.s1, own.r1, own.r2, own.r3 = work.s1, work.r1, work.r2, work.r3
        reductions.append(Reduction(place, i, own, sems))
    fout, fin, tout, tqkv, sout, sqkv = reductions
    small = SmallSums(place, work, sum_sems)

    def tall(source, base, index):
        slot = (base + index) % SLOTS
        rows = pl.ds(pl.multiple_of(index * HIDE, HIDE), HIDE)
        return pltpu.make_async_copy(source.at[rows], work.tall.at[slot], ring_sems.at[0, slot])

    def broad(source, base, index):
        slot = (base + index) % SLOTS
        return pltpu.make_async_copy(
            source.at[:, lanes(index, HIDE)], work.broad.at[slot], ring_sems.at[1, slot]
        )

    def slope(base, index):
        slot = (base + index) % SLOTS
        return pltpu.make_async_copy(saved.slope.at[index], work.slope_in.at[slot], ring_sems.at[2, slot])

    def record(source, base, index):
        slot = (base + index) % SLOTS
        return pltpu.make_async_copy(
            source.at[index], work.record.at[slot, pl.ds(0, source.shape[1])], ring_sems.at[3, slot]
        )

    def open_stream(maker, count):
        for index in range(min(SLOTS, count)):
            maker(index).start()

    def refill(maker, count, index):
        @pl.when(index + SLOTS < count)
        def _():
            maker(index + SLOTS).start()

    fout_tiles = functools.partial(tall, weights.w_fout, 0)
    tout_tiles = functools.partial(tall, weights.w_tout, 8)
    sout_tiles = functools.partial(tall, weights.w_sout, 10)
    fin_tiles = functools.partial(broad, weights.w_fin, 0)
    tqkv_tiles = functools.partial(broad, weights.w_tqkv, 8)
    sqkv_tiles = functools.partial(broad, weights.w_sqkv, 14)
    slopes = functools.partial(slope, 0)
    temporal_records = functools.partial(record, saved.temporal, 0)
    spatial_records = functools.partial(record, saved.spatial, 8)

    class Kept:
        def __init__(self, normals, scales):
            self.copies = (
                pltpu.make_async_copy(normals, work.resid, io_sems.at[0]),
                pltpu.make_async_copy(scales, work.scale, io_sems.at[4]),
            )
            for copy in self.copies:
                copy.start()

        def wait(self):
            for copy in self.copies:
                copy.wait()

    open_stream(fout_tiles, 8)
    open_stream(slopes, 8)
    open_stream(fin_tiles, 8)
    kept3 = Kept(saved.normal3, saved.scale3)
    open_stream(temporal_records, 8)
    work.sums[...] = jnp.zeros_like(work.sums)
    for row, gain in enumerate(gains):
        work.gains[row : row + 1] = gain[...].astype(F32).reshape(1, WIDTH)
    greet(place, True)
    for one in reductions:
        one.lefts()

    grad, total = work.grad, work.total

    def start_rows(step, carry):
        near = pl.ds(pl.multiple_of(step * 16, 16), 16)
        big = ins.big_cot[near].astype(F32)
        little = ins.small_cot[near].astype(F32) * ins.live[step // 2].astype(F32)
        merged = interleave(big, little)
        rows = pl.ds(pl.multiple_of(step * 32, 32), 32)
        grad[rows] = merged
        work.low3[rows] = merged.astype(BF16)
        total[rows] = jnp.zeros_like(merged)
        work.sums[OUTER : OUTER + 1] += jnp.sum(merged, axis=0, keepdims=True)
        return carry

    lax.fori_loop(0, 8, start_rows, 0)
    fout.rights()

    def feed(step, carry):
        slopes(step).wait()
        fout_tiles(step).wait()
        fin_tiles(step).wait()
        slot = step % SLOTS
        down = dot_nt(work.low3[...], work.tall[slot]) * work.slope_in[slot].astype(F32)
        work.inner_sums[pl.ds(step, 1)] = jnp.sum(down, axis=0, keepdims=True)
        low = down.astype(BF16)
        work.hidden_low[:, lanes(step, HIDE)] = low
        for column in range(WIDTH // 256):
            at = slice(column * 256, column * 256 + 256)
            total[:, at] += dot_nt(low, work.broad[slot, at])
        refill(slopes, 8, step)
        refill(fout_tiles, 8, step)
        refill(fin_tiles, 8, step)
        return carry

    lax.fori_loop(0, 4, feed, 0)
    fout.loaded()
    fout.first()
    lax.fori_loop(4, 8, feed, 0)
    fin.rights()
    open_stream(tout_tiles, 2)
    open_stream(sout_tiles, 1)
    open_stream(tqkv_tiles, 6)
    for part in range(PAIRS):
        at = part % 2 * HIDE
        work.sums[INNER + part // 2 : INNER + part // 2 + 1, at : at + HIDE] = work.inner_sums[part : part + 1]

    def norm_back(gradient, gain_row, row, low, bias_row):
        gain = work.gains[gain_row : gain_row + 1]

        def one(step, carry):
            rows = rows16(step)
            error = gradient[rows].astype(F32)
            normal, scale = work.resid[rows], work.scale[rows, 0:1]
            scaled = error * gain
            mean_one = jnp.mean(scaled, axis=-1, keepdims=True)
            mean_two = jnp.mean(scaled * normal, axis=-1, keepdims=True)
            value = grad[rows] + (scaled - mean_one - normal * mean_two) * scale
            grad[rows] = value
            if low is not None:
                low[rows] = value.astype(BF16)
            gains = error * normal
            sums = [part[:8] + part[8:] for part in (gains, error, value)]
            return tuple(a + b for a, b in zip(carry, sums))

        zero = jnp.zeros((8, WIDTH), F32)
        sums = lax.fori_loop(0, 16, one, (zero, zero, zero), unroll=2)
        work.sums[row : row + 1] = jnp.sum(sums[0], axis=0, keepdims=True)
        work.sums[row + 1 : row + 2] = jnp.sum(sums[1], axis=0, keepdims=True)
        if bias_row is not None:
            work.sums[bias_row : bias_row + 1] = jnp.sum(sums[2], axis=0, keepdims=True)

    kept3.wait()
    norm_back(total, 2, GAIN3, work.low2, TEMPORAL_BIAS)
    kept2 = Kept(saved.normal2, saved.scale2)
    tout.rights()

    there = [Swap(place, work.swap_send, work.context_back, swap_sems, i, True, HALVES[i]) for i in range(2)]
    for index in range(2):
        tout_tiles(index).wait()
        slot = (8 + index) % SLOTS
        work.swap_send[:, HALVES[index]] = dot_nt(work.low2[...], work.tall[slot]).astype(BF16)
        there[index].start()
    sout_tiles(1).start()
    fout.pass_on()
    fin.loaded()
    fin.first()
    there[0].wait()

    low_lanes = half_masks(128)
    low_lanes_wide = half_masks(256)

    def attention_back(probs, keys, values, queries, upstream, wide):
        key_low = low_lanes_wide if wide else low_lanes
        upstreams = by_head(upstream, low_lanes)
        errors = []
        for head in range(2):
            prob = probs[head].astype(F32)
            back = dot_nt(values, upstreams[head])
            delta = jnp.sum(prob * back, axis=0, keepdims=True)
            errors.append((prob * (back - delta)).astype(BF16))
        key_grad = dot(jnp.concatenate(errors, axis=1), jnp.concatenate(by_head(queries, low_lanes), axis=0))
        value_grad = dot(jnp.concatenate(probs, axis=1), jnp.concatenate(upstreams, axis=0))
        query_grad = dot_tn(jnp.concatenate(errors, axis=0), jnp.concatenate(by_head(keys, key_low), axis=0))
        return query_grad * 0.125, key_grad, value_grad

    def temporal_pair(pair, carry):
        temporal_records(pair).wait()
        slot = pair % SLOTS
        for half in range(2):
            base = half * 128

            def rows(start, half=half):
                return work.record[slot, start + half * 128 : start + half * 128 + 128]

            probs = [work.record[slot, (half * 2 + h) * 128 : (half * 2 + h) * 128 + 128] for h in range(2)]
            upstream = work.context_back[base : base + 128, lanes(pair, LANES)]
            grads = attention_back(probs, rows(TP_KEY), rows(TP_VALUE), rows(TP_QUERY), upstream, False)
            for i, value in enumerate(grads):
                work.packed[base : base + 128, lanes(pair + i * PAIRS, LANES)] = value.astype(BF16)
        refill(temporal_records, 8, pair)
        return carry

    lax.fori_loop(0, PAIRS // 2, temporal_pair, 0)
    there[1].wait()
    lax.fori_loop(PAIRS // 2, PAIRS, temporal_pair, 0)
    open_stream(spatial_records, 8)
    tqkv.rights()
    fin.pass_on()

    def project_back(maker, base, start, stop):
        def one(step, carry):
            maker(step).wait()
            slot = (base + step) % SLOTS
            low = work.packed[:, lanes(step, HIDE)]
            for column in range(WIDTH // 256):
                at = slice(column * 256, column * 256 + 256)
                value = dot_nt(low, work.broad[slot, at])
                total[:, at] += value
            refill(maker, 6, step)
            return carry

        if start == 0:
            total[...] = jnp.zeros_like(total)
        lax.fori_loop(start, stop, one, 0)

    project_back(tqkv_tiles, 8, 0, 6)
    open_stream(sqkv_tiles, 6)
    for one in there:
        one.sent()
    work.swap_send[...] = total[...].astype(BF16)
    back = Swap(place, work.swap_send, work.normed_back, swap_sems, 2, False)
    back.start()
    fout.second()
    fout.first_sent()
    tout.loaded()
    tout.first()
    back.wait()

    kept2.wait()
    norm_back(work.normed_back, 1, GAIN2, work.low1, SPATIAL_BIAS)
    kept1 = Kept(saved.normal1, saved.scale1)
    sout.rights()
    for index in range(2):
        sout_tiles(index).wait()
        slot = (10 + index) % SLOTS
        at = slice(index * HIDE, index * HIDE + HIDE)
        value = dot_nt(work.low1[...], work.tall[slot])
        for which in range(2):
            work.context_grad[which, :, at] = family(value, which).astype(BF16)
    tqkv.rights_sent()
    tqkv.loaded()
    tqkv.first()
    fin.second()
    tout.pass_on()

    def spatial_pair(pair, carry):
        spatial_records(pair).wait()
        slot = (8 + pair) % SLOTS
        all_grads = []
        for which in range(2):

            def rows(start, count, which=which):
                return work.record[slot, start + which * count : start + which * count + count]

            probs = [work.record[slot, (which * 2 + h) * 256 : (which * 2 + h) * 256 + 256] for h in range(2)]
            upstream = work.context_grad[which, :, lanes(pair, LANES)]
            all_grads.append(
                attention_back(
                    probs, rows(SP_KEY, 256), rows(SP_VALUE, 256), rows(SP_QUERY, 128), upstream, True
                )
            )
        for i in range(3):
            value = interleave(all_grads[0][i][:128], all_grads[1][i][:128])
            work.packed[:, lanes(pair + i * PAIRS, LANES)] = value.astype(BF16)
        for i in (1, 2):
            value = interleave(all_grads[0][i][128:], all_grads[1][i][128:])
            work.far_send[:, lanes(pair + (i - 1) * PAIRS, LANES)] = value.astype(BF16)
        refill(spatial_records, 8, pair)
        return carry

    lax.fori_loop(0, PAIRS, spatial_pair, 0)
    far = remote(work.far_send, work.far_recv, far_sems.at[0], far_sems.at[1], place.partner)
    far.start()
    tqkv.pass_on()
    fin.first_sent()
    sout.loaded()
    sout.first()
    fout.third()
    far.wait()

    def join(step, carry):
        rows = rows16(step)
        value = work.packed[rows, WIDTH:].astype(F32) + work.far_recv[rows].astype(F32)
        work.packed[rows, WIDTH:] = value.astype(BF16)
        return carry

    lax.fori_loop(0, 16, join, 0)
    sqkv.rights()
    project_back(sqkv_tiles, 14, 0, 2)
    sqkv.loaded()
    sqkv.first()
    project_back(sqkv_tiles, 14, 2, 6)
    sqkv.pass_on()
    sout.pass_on()
    tout.second()
    tqkv.second()
    kept1.wait()
    norm_back(total, 0, GAIN1, None, None)
    fin.third()

    def finish_rows(step, carry):
        value = grad[pl.ds(pl.multiple_of(step * 32, 32), 32)]
        big, little = family(value, 0), family(value, 1)
        near = pl.ds(pl.multiple_of(step * 16, 16), 16)
        total[near] = big
        total[pl.ds(pl.multiple_of(128 + step * 16, 16), 16)] = little
        work.frame_sums[0:1] += jnp.sum(big, axis=0, keepdims=True)
        work.frame_sums[pl.ds(1 + step // 2, 1)] += jnp.sum(little, axis=0, keepdims=True)
        return carry

    work.frame_sums[...] = jnp.zeros_like(work.frame_sums)
    lax.fori_loop(0, 8, finish_rows, 0)
    out_copies = [
        pltpu.make_async_copy(total.at[:128], outs.big_grad, io_sems.at[1]),
        pltpu.make_async_copy(total.at[128:], outs.small_grad, io_sems.at[2]),
    ]
    for copy in out_copies:
        copy.start()
    table, at_row = jnp.zeros((8, WIDTH), F32), lax.broadcasted_iota(jnp.int32, (8, WIDTH), 0)
    for i in range(5):
        action = ins.big_actions[0, frame] if i == 0 else ins.small_actions[i - 1, frame]
        table = table + jnp.where(at_row == action, work.frame_sums[i : i + 1], 0.0)
    work.sums[0:8] = table
    small.begin()
    fout.fourth()
    sout.second()
    small.step0()
    tout.third()
    fin.fourth()
    sqkv.second()
    small.advance(0)
    tqkv.third()
    sout.third()
    small.advance(1)
    fout.fifth()
    sqkv.third()
    tout.fourth()
    fin.fifth()
    small.advance(2)
    tqkv.fourth()
    sout.fourth()
    sqkv.fourth()
    tout.fifth()
    tqkv.fifth()
    sout.fifth()
    sqkv.fifth()
    small.finish(outs.small_sums, io_sems.at[3])
    for one in reductions:
        one.finish()
    for one in (tout, tqkv, sout, sqkv):
        one.first_sent()
    for one in (fout, fin, tout, sout, sqkv):
        one.rights_sent()
    back.sent()
    for copy in out_copies:
        copy.wait()


def backward(ins, scalars, gains, lefts, saved, weights):
    sem = pltpu.SemaphoreType.DMA
    count = len(MATRICES)
    work = [pltpu.VMEM(shape, dtype) for shape, dtype in BACK_WORK.values()]
    work += [pltpu.VMEM((2, 4, 2, 4, k // 64, 2 * ROWS), BF16) for k, _, _ in MATRICES]
    work += [pltpu.VMEM((2 * ROWS, n // 2), BF16) for _, n, _ in MATRICES]
    work += [pltpu.VMEM((k // 64, n // 2), BF16) for k, n, _ in MATRICES]
    work += [sem(shape) for shape in BACK_SEMS.values()]
    shapes = list(BACK_OUTS.values()) + [((k // 8, n), BF16) for k, n, _ in MATRICES]
    in_keys, saved_keys, weight_keys = tuple(vars(ins)) + tuple(vars(scalars)), tuple(vars(saved)), tuple(vars(weights))
    return pl.pallas_call(
        functools.partial(backward_kernel, in_keys, saved_keys, weight_keys),
        out_shape=[jax.ShapeDtypeStruct(shape, dtype) for shape, dtype in shapes],
        in_specs=[VMEM] * len(vars(ins))
        + [SMEM] * len(vars(scalars))
        + [VMEM] * len(gains)
        + [ANY] * (count + len(saved_keys) + len(weight_keys)),
        out_specs=[ANY] * len(shapes),
        scratch_shapes=work,
        compiler_params=pltpu.CompilerParams(
            collective_id=2, has_side_effects=True, vmem_limit_bytes=63 * 2**20
        ),
        cost_estimate=pl.CostEstimate(flops=18 * 10**9, bytes_accessed=80 * 2**20, transcendentals=0),
        name="layer_backward",
    )(
        *vars(ins).values(),
        *vars(scalars).values(),
        *gains,
        *[left.reshape(2, 4, 2, 4, k // 64, ROWS) for left, (k, _, _) in zip(lefts, MATRICES)],
        *vars(saved).values(),
        *vars(weights).values(),
    )


SUM_VECTORS = (
    (GAIN1, 1),
    (SHIFT1, 1),
    (SPATIAL_BIAS, 1),
    (GAIN2, 1),
    (SHIFT2, 1),
    (TEMPORAL_BIAS, 1),
    (GAIN3, 1),
    (SHIFT3, 1),
    (INNER, 4),
    (OUTER, 1),
)


def widen_kernel(*refs):
    refs = list(refs)
    count, passed = len(MATRICES), 4
    narrow = [refs.pop(0) for _ in range(count)]
    plain = [refs.pop(0) for _ in range(passed)]
    sums = refs.pop(0)
    wide = [refs.pop(0) for _ in range(count)]
    plain_out = [refs.pop(0) for _ in range(passed)]
    table, vectors = refs.pop(0), [refs.pop(0) for _ in SUM_VECTORS]
    narrow_in, wide_out = refs[:count], refs[count : 2 * count]
    sems = refs[2 * count]
    loads = [pltpu.make_async_copy(narrow[i], narrow_in[i], sems.at[0, i]) for i in range(count)]
    stores = [pltpu.make_async_copy(wide_out[i], wide[i], sems.at[1, i]) for i in range(count)]
    moves = [pltpu.make_async_copy(plain[i], plain_out[i], sems.at[2, i]) for i in range(passed)]
    for copy in loads + moves:
        copy.start()
    table[...] = sums[0:8]
    for (row, rows), vector in zip(SUM_VECTORS, vectors):
        for i in range(rows):
            vector[i * WIDTH : (i + 1) * WIDTH] = sums[row + i]
    for i in range(count):
        loads[i].wait()

        def one(step, carry, i=i):
            wide_out[i][rows16(step)] = narrow_in[i][rows16(step)].astype(F32)
            return carry

        lax.fori_loop(0, narrow_in[i].shape[0] // 16, one, 0, unroll=2)
        stores[i].start()
    for copy in stores + moves:
        copy.wait()


def widen(matrices, plain, sums):
    count = len(matrices)
    vectors = [jax.ShapeDtypeStruct((rows * WIDTH,), F32) for _, rows in SUM_VECTORS]
    shapes = [jax.ShapeDtypeStruct(one.shape, F32) for one in matrices]
    scratch = [pltpu.VMEM(one.shape, BF16) for one in matrices] + [pltpu.VMEM(one.shape, F32) for one in matrices]
    results = pl.pallas_call(
        widen_kernel,
        out_shape=shapes
        + [jax.ShapeDtypeStruct(one.shape, one.dtype) for one in plain]
        + [jax.ShapeDtypeStruct((8, WIDTH), F32)]
        + vectors,
        in_specs=[ANY] * (count + len(plain)) + [VMEM],
        out_specs=[ANY] * (count + len(plain)) + [VMEM] * (1 + len(vectors)),
        scratch_shapes=scratch + [pltpu.SemaphoreType.DMA((3, count))],
        compiler_params=pltpu.CompilerParams(vmem_limit_bytes=62 * 2**20),
        cost_estimate=pl.CostEstimate(flops=0, bytes_accessed=14 * 2**20, transcendentals=0),
        name="widen",
    )(*matrices, *plain, sums)
    results = list(results)
    wide = [results.pop(0) for _ in range(count)]
    passed = [results.pop(0) for _ in plain]
    return wide, passed, results


def body(
    big_tokens,
    small_tokens,
    big_actions,
    small_actions,
    big_order,
    small_order,
    small_live,
    action_table,
    norm1_gain,
    norm1_bias,
    spatial_qkv,
    spatial_out,
    spatial_out_bias,
    norm2_gain,
    norm2_bias,
    temporal_qkv,
    temporal_out,
    temporal_out_bias,
    norm3_gain,
    norm3_bias,
    ffn_in,
    ffn_in_bias,
    ffn_out,
    ffn_out_bias,
    big_cotangent,
    small_cotangent,
):
    scalars = Names(
        big_actions=big_actions,
        small_actions=small_actions,
        big_order=big_order,
        small_order=small_order,
        live=small_live,
    )
    vectors = (
        norm1_gain,
        norm1_bias,
        spatial_out_bias,
        norm2_gain,
        norm2_bias,
        temporal_out_bias,
        norm3_gain,
        norm3_bias,
        ffn_out_bias,
    )
    weights = Names(
        w_sqkv=spatial_qkv,
        w_sout=spatial_out,
        w_tqkv=temporal_qkv,
        w_tout=temporal_out,
        w_fin=ffn_in,
        w_fout=ffn_out,
    )
    saved = forward(
        Names(
            big=big_tokens.reshape(128, WIDTH),
            small=small_tokens.reshape(128, WIDTH),
            table=action_table,
            inner_bias=ffn_in_bias,
        ),
        scalars,
        vectors,
        weights,
    )
    big_grad, small_grad, sums, *matrices = backward(
        Names(big_cot=big_cotangent.reshape(128, WIDTH), small_cot=small_cotangent.reshape(128, WIDTH)),
        Names(big_actions=big_actions, small_actions=small_actions, live=small_live),
        (norm1_gain, norm2_gain, norm3_gain),
        (saved.activated_t, saved.normed3_t, saved.context2_t, saved.normed2_t, saved.context1_t, saved.normed1_t),
        Names(
            normal1=saved.normal1,
            normal2=saved.normal2,
            normal3=saved.normal3,
            scale1=saved.scale1,
            scale2=saved.scale2,
            scale3=saved.scale3,
            spatial=saved.spatial,
            temporal=saved.temporal,
            slope=saved.slope,
        ),
        weights,
    )
    matrices, passed, small = widen(matrices, (saved.big_out, saved.small_out, big_grad, small_grad), sums)
    g_fout, g_fin, g_tout, g_tqkv, g_sout, g_sqkv = matrices
    table, gain1, shift1, bias_s, gain2, shift2, bias_t, gain3, shift3, bias_in, bias_out = small
    return (
        passed[0].reshape(1, 128, WIDTH),
        passed[1].reshape(4, 32, WIDTH),
        passed[2].reshape(1, 128, WIDTH),
        passed[3].reshape(4, 32, WIDTH),
        table,
        gain1,
        shift1,
        g_sqkv,
        g_sout,
        bias_s,
        gain2,
        shift2,
        g_tqkv,
        g_tout,
        bias_t,
        gain3,
        shift3,
        g_fin,
        bias_in,
        g_fout,
        bias_out,
    )


def solution(mesh):
    spread, by_col = P("col", "ta", None), P("col", None)
    return jax.shard_map(
        body,
        mesh=mesh,
        in_specs=(spread, spread, by_col, by_col, by_col, by_col, P("col")) + (P(),) * 17 + (spread, spread),
        out_specs=(spread,) * 4
        + (P(),) * 3
        + (by_col, by_col, P(), P(), P(), by_col, by_col, P(), P(), P(), by_col, P(), by_col, P()),
        check_vma=False,
    )
```

time: 436 us -> 261 us (0.60); the launches traced: 428 us -> 260 us
  Pallas kernels: 126 us -> 260 us
  local copies, waits for them, and re-layouts: 109 us -> 0 us
  matrix products: 70.3 us -> 0 us
  other arithmetic: 39.3 us -> 0 us
  waiting for transfers between devices: 39 us -> 0 us
  starting transfers between devices: 28.8 us -> 0 us
  between operations: 15.6 us -> 0.86 us
    pallas_call x1 -> x3, Pallas kernels: 126 us -> 260 us  [the longest x1 143 us: backward(): pl.pallas_call(functools.partial(backward_kernel, in_keys, saved_keys, we...]
    dot_general x25 -> x0, matrix products: 70.3 us -> none  [the longest x6 25 us: project(): jnp.einsum('...k,kn->...n', activation, weight, preferred_element_type=jn...]
    all_to_all x4 -> x0, starting transfers between devices: 25.8 us -> none  [the longest x2 13.2 us: to_positions(): lax.all_to_all(blocks, 'ta', split_axis=0, concat_axis=0, tiled=True)]
    convert_element_type x15 -> x0, local copies, waits for them, and re-layouts: 24.4 us -> none  [the longest x12 19.8 us: reduce_gradients(): finished.append(value.astype(jnp.float32))]
    all_to_all x4 -> x0, waiting for transfers between devices: 21.2 us -> none  [the longest x2 10.8 us: to_positions(): lax.all_to_all(blocks, 'ta', split_axis=0, concat_axis=0, tiled=True)]
    concatenate x10 -> x0, local copies, waits for them, and re-layouts: 20.4 us -> none  [the longest x6 13.1 us: body(): jnp.concatenate([g.reshape(2, 128, width) for g in grads], axis=-1)]
    convert_element_type x23 -> x0, other arithmetic: 16.9 us -> none  [the longest x4 5.9 us: reduce_gradients(): finished.append(value.astype(jnp.float32))]
    psum x1 -> x0, waiting for transfers between devices: 16.3 us -> none  [body(): small = lax.psum(small, ('ta', 'col'))]
  transfers between devices with their start and end apart: 7 -> 0, of which waited for: 5 -> 0; matrix products, arithmetic and copies ran while one was open for 20% -> 0% of each run, Pallas kernels for 29% -> 0%
where the time goes in v2:
time: 261 us; the launch traced here: 260 us
  Pallas kernels  260 us (100%)
    pallas_call x1, Pallas kernels, backward(): pl.pallas_call(functools.partial(backward_kernel, in_keys, saved_keys, we...  143 us
    pallas_call x1, Pallas kernels, forward(): pl.pallas_call(functools.partial(forward_kernel, in_keys, len(vectors), w...  66.2 us
    pallas_call x1, Pallas kernels, widen(): pl.pallas_call(widen_kernel, out_shape=shapes + [jax.ShapeDtypeStruct(one...  50.5 us

profile of v2, /device:TPU:1, one launch (start us, length us, event | category | flops | bytes accessed | tf_op | source)
XLA Modules:
  0.0 260.5 jit_solution(5348583092431825248)
XLA Ops:
  0.7 66.2 %layer_forward.1 = (bf16[128,1024]{1,0:T(8,128)(2,1)}, bf16[128,1024]{1,0:T(8,128)(2,1)}, f32[256,1024]{1,0:T(8,128)}, f32[256,1024]{1,0:T(8,128)}, f32[256,1024...) custom-call(bf16[128,1024]{1,0:T(8,128)(2,1)} %bitcast.14, ...), custom_call_target="tpu_custom_call" | custom-call | flops 8999999488 | bytes 62914560 | tf_op jit(solution)/shard_map/layer_forward/pallas_call | solution.py:533
  66.9 142.9 %layer_backward.1 = (f32[128,1024]{1,0:T(8,128)}, f32[128,1024]{1,0:T(8,128)}, f32[32,1024]{1,0:T(8,128)}, bf16[512,1024]{1,0:T(8,128)(2,1)}, bf16[128,4096]{1,0...) custom-call(bf16[128,1024]{1,0:T(8,128)(2,1)} %bitcast.24, ...), custom_call_target="tpu_custom_call" | custom-call | flops 17999998976 | bytes 83886080 | tf_op jit(solution)/shard_map/layer_backward/pallas_call | solution.py:1313
  209.8 50.5 %widen.1 = (f32[512,1024]{1,0:T(8,128)}, f32[128,4096]{1,0:T(8,128)}, f32[128,1024]{1,0:T(8,128)}, f32[128,3072]{1,0:T(8,128)}, f32[128,1024]{1,0:T(8,128)}, /*i...) custom-call(bf16[512,1024]{1,0:T(8,128)(2,1)} %get-tuple-element.83., ...), custom_call_target="tpu_custom_call" | custom-call | bytes 14680064 | tf_op jit(solution)/shard_map/widen/pallas_call | solution.py:1389

commit v3 on v2

--- a/solution.py
+++ b/solution.py
@@ -27,12 +27,13 @@
 ORDERS = (("x", "y", "z"), ("y", "z", "x"), ("z", "x", "y"))
 MATRICES = (
     (HIDDEN, WIDTH, (1, 1, 2)),
-    (WIDTH, HIDDEN, (6, 6, 4)),
-    (WIDTH, WIDTH, (1, 2, 1)),
+    (WIDTH, HIDDEN, (4, 6, 6)),
+    (WIDTH, WIDTH, (1, 1, 2)),
     (WIDTH, 3 * WIDTH, (4, 4, 4)),
-    (WIDTH, WIDTH, (2, 1, 1)),
+    (WIDTH, WIDTH, (1, 1, 2)),
     (WIDTH, 3 * WIDTH, (4, 4, 4)),
 )
+ALL, XY, Z = (0, 1, 2), (0, 1), (2,)
 SEND_UNITS = (0, 16, 12, 0, 28, 16)
 
 
@@ -561,6 +562,7 @@
         self.first_unit = sum(m[1] // 2 // LANES * (m[0] // 1024) for m in MATRICES[:index])
         self.send_unit = SEND_UNITS[index]
         self.local_done = False
+        self.straight = index >= 4
 
     def left_local(self):
         r, s, i = self.refs, self.sems, self.index
@@ -665,9 +667,9 @@
         target = r.r1.at[way, here]
         return remote(source, target, s.send.at[i, part, 0, 2 + way], s.recv.at[i, part, 0, 2 + way], device)
 
-    def first(self):
+    def first(self, parts=ALL):
         r = self.refs
-        for part in range(3):
+        for part in parts:
             slot = self.place.along(ORDERS[part][0], 2)[1]
 
             def emit(unit, value):
@@ -677,9 +679,9 @@
             for way in range(2):
                 self.relay(part, way).start()
 
-    def pass_on(self):
+    def pass_on(self, parts=ALL):
         r = self.refs
-        for part in range(3):
+        for part in parts:
             for way in range(2):
                 self.relay(part, way).wait_recv()
                 slot = self.place.along(ORDERS[part][0], 3 if way else 1)[1]
@@ -696,15 +698,19 @@
                 self.products(part, slot, emit)
                 self.direct(part, way).start()
 
-    def first_sent(self):
+    def relay_sent(self):
         for part in range(3):
             for way in range(2):
                 self.relay(part, way).wait_send()
+
+    def direct_sent(self):
+        for part in range(3):
+            for way in range(2):
                 self.direct(part, way).wait_send()
 
-    def second(self):
+    def second(self, parts=ALL):
         r = self.refs
-        for part in range(3):
+        for part in parts:
             slot = self.place.along(ORDERS[part][0], 0)[1]
             for way in range(2):
                 self.direct(part, way).wait_recv()
@@ -719,9 +725,9 @@
             for step in (1, 2, 3):
                 self.copy(part, 1, step).start()
 
-    def third(self):
+    def third(self, parts=ALL):
         r = self.refs
-        for part in range(3):
+        for part in parts:
             slot = self.place.along(ORDERS[part][1], 0)[1]
             for step in (1, 2, 3):
                 self.copy(part, 1, step).wait_recv()
@@ -741,20 +747,32 @@
     def mine(self):
         return self.place.y_hi * 4 + self.place.x
 
-    def rows_of(self, slot):
-        return pl.ds(pl.multiple_of(slot * self.depth, self.depth), self.depth)
-
     def gather_copy(self, y_hi, x, slot):
         r, s, i, place = self.refs, self.sems, self.index, self.place
-        target = r.out.at[self.rows_of(slot), lanes(place.core, self.half)]
+        target = r.out.at[slot // 4, slot % 4, :, lanes(place.core, self.half)]
         return remote(
-            r.piece, target, s.ag_send.at[i, y_hi * 4 + x], s.ag_recv.at[i, slot],
+            r.piece.at[place.y_hi], target, s.ag_send.at[i, y_hi * 4 + x], s.ag_recv.at[i, slot],
             place.device(y_hi=y_hi, x=x),
         )
 
+    def twin_copy(self):
+        r, s, i, place = self.refs, self.sems, self.index, self.place
+        block = r.piece.at[place.y_hi]
+        return remote(block, block, s.ag_send.at[i, 0], s.ag_recv.at[i, 0], place.device(y_hi=1 - place.y_hi))
+
+    def line_copy(self, step):
+        r, s, i, place = self.refs, self.sems, self.index, self.place
+        target = r.out.at[:, place.x, :, lanes(place.core, self.half)]
+        device = place.device(x=(place.x + step) % 4)
+        return remote(r.piece, target, s.ag_send.at[i, step], s.ag_recv.at[i, step], device)
+
     def own_copy(self):
-        target = self.refs.out.at[self.rows_of(self.mine()), lanes(self.place.core, self.half)]
-        return pltpu.make_async_copy(self.refs.piece, target, self.sems.local.at[self.index, 2])
+        place, i, piece = self.place, self.index, self.refs.piece
+        columns = lanes(place.core, self.half)
+        if self.straight:
+            target = self.refs.out.at[place.y_hi, place.x, :, columns]
+            return pltpu.make_async_copy(piece.at[place.y_hi], target, self.sems.local.at[i, 2])
+        return pltpu.make_async_copy(piece, self.refs.out.at[:, place.x, :, columns], self.sems.local.at[i, 2])
 
     def others(self):
         place = self.place
@@ -764,9 +782,9 @@
                 if y_step or x_step:
                     yield y_hi, (place.x + x_step) % 4
 
-    def fourth(self):
+    def fourth(self, parts=ALL):
         r = self.refs
-        for part in range(3):
+        for part in parts:
             slot = self.place.along(ORDERS[part][2], 0)[1]
             for step in (1, 2, 3):
                 self.copy(part, 2, step).wait_recv()
@@ -777,27 +795,48 @@
                 for i in range(3):
                     value = value + r.r3[i, at].astype(F32)
                 tile, group = unit // self.groups, unit % self.groups
-                r.piece[group * 16 : group * 16 + 16, tile * LANES : tile * LANES + LANES] = value.astype(BF16)
-        self.own_copy().start()
-        for y_hi, x in self.others():
-            self.gather_copy(y_hi, x, self.mine()).start()
+                rows, columns = slice(group * 16, group * 16 + 16), slice(tile * LANES, tile * LANES + LANES)
+                r.piece[self.place.y_hi, rows, columns] = value.astype(BF16)
+    def gather(self):
+        if self.straight:
+            self.own_copy().start()
+            for y_hi, x in self.others():
+                self.gather_copy(y_hi, x, self.mine()).start()
+        else:
+            self.twin_copy().start()
+
+    def spread(self):
+        if not self.straight:
+            self.twin_copy().wait_recv()
+            self.own_copy().start()
+            for step in (1, 2, 3):
+                self.line_copy(step).start()
 
     def cross_copy(self):
         r, s, i, core = self.refs, self.sems, self.index, self.place.core
-        block = r.out.at[:, lanes(core, self.half)]
+        block = r.out.at[:, :, :, lanes(core, self.half)]
         return remote(block, block, s.cross.at[i, 0], s.cross.at[i, 1], self.place.partner)
 
     def fifth(self):
         self.own_copy().wait()
-        for y_hi, x in self.others():
-            self.gather_copy(y_hi, x, y_hi * 4 + x).wait_recv()
+        if self.straight:
+            for y_hi, x in self.others():
+                self.gather_copy(y_hi, x, y_hi * 4 + x).wait_recv()
+        else:
+            for step in (1, 2, 3):
+                self.line_copy(step).wait_recv()
         self.cross_copy().start()
 
     def finish(self):
         self.cross_copy().wait()
         self.left_far().wait_send()
-        for y_hi, x in self.others():
-            self.gather_copy(y_hi, x, self.mine()).wait_send()
+        if self.straight:
+            for y_hi, x in self.others():
+                self.gather_copy(y_hi, x, self.mine()).wait_send()
+        else:
+            self.twin_copy().wait_send()
+            for step in (1, 2, 3):
+                self.line_copy(step).wait_send()
         for part in range(3):
             for stage in (1, 2):
                 for step in (1, 2, 3):
@@ -812,7 +851,7 @@
         self.place, self.refs, self.sems = place, refs, sems
 
     def share(self, core):
-        return pl.ds(pl.multiple_of(core * 16, 16), 16)
+        return slice(None), lanes(core, WIDTH // 2)
 
     def cross(self):
         r, core = self.refs, self.place.core
@@ -869,7 +908,7 @@
 BACK_OUTS = dict(
     big_grad=((128, WIDTH), F32),
     small_grad=((128, WIDTH), F32),
-    small_sums=((32, WIDTH), F32),
+    small_sums=((24, WIDTH), F32),
 )
 SLOTS = 3
 BACK_WORK = dict(
@@ -896,11 +935,11 @@
     far_send=((ROWS, 2 * WIDTH), BF16),
     far_recv=((ROWS, 2 * WIDTH), BF16),
     inner_sums=((PAIRS, HIDE), F32),
-    sums=((32, WIDTH), F32),
-    sums_core=((16, WIDTH), F32),
-    sums_total=((3, 16, WIDTH), F32),
-    sums_recv=((3, 3, 16, WIDTH), F32),
-    sums_final=((32, WIDTH), F32),
+    sums=((24, WIDTH), F32),
+    sums_core=((24, WIDTH // 2), F32),
+    sums_total=((3, 24, WIDTH // 2), F32),
+    sums_recv=((3, 3, 24, WIDTH // 2), F32),
+    sums_final=((24, WIDTH), F32),
     frame_sums=((8, WIDTH), F32),
     scale=((ROWS, LANES), F32),
     gains=((8, WIDTH), F32),
@@ -1095,10 +1134,12 @@
         work.swap_send[:, HALVES[index]] = dot_nt(work.low2[...], work.tall[slot]).astype(BF16)
         there[index].start()
     sout_tiles(1).start()
-    fout.pass_on()
+    fout.pass_on(Z)
     fin.loaded()
-    fin.first()
+    fin.first(Z)
     there[0].wait()
+    fout.pass_on(XY)
+    fin.first(XY)
 
     low_lanes = half_masks(128)
     low_lanes_wide = half_masks(256)
@@ -1139,7 +1180,6 @@
     lax.fori_loop(PAIRS // 2, PAIRS, temporal_pair, 0)
     open_stream(spatial_records, 8)
     tqkv.rights()
-    fin.pass_on()
 
     def project_back(maker, base, start, stop):
         def one(step, carry):
@@ -1157,18 +1197,27 @@
             total[...] = jnp.zeros_like(total)
         lax.fori_loop(start, stop, one, 0)
 
-    project_back(tqkv_tiles, 8, 0, 6)
+    project_back(tqkv_tiles, 8, 0, 3)
+    fin.pass_on(Z)
+    fout.relay_sent()
+    tout.loaded()
+    tout.first()
+    tqkv.loaded()
+    tqkv.first()
+    project_back(tqkv_tiles, 8, 3, 6)
     open_stream(sqkv_tiles, 6)
     for one in there:
         one.sent()
     work.swap_send[...] = total[...].astype(BF16)
     back = Swap(place, work.swap_send, work.normed_back, swap_sems, 2, False)
     back.start()
-    fout.second()
-    fout.first_sent()
-    tout.loaded()
-    tout.first()
+    fout.second((1,))
+    fout.direct_sent()
     back.wait()
+    tout.pass_on()
+    tqkv.pass_on()
+    fin.pass_on(XY)
+    fout.second((0, 2))
 
     kept2.wait()
     norm_back(work.normed_back, 1, GAIN2, work.low1, SPATIAL_BIAS)
@@ -1182,10 +1231,6 @@
         for which in range(2):
             work.context_grad[which, :, at] = family(value, which).astype(BF16)
     tqkv.rights_sent()
-    tqkv.loaded()
-    tqkv.first()
-    fin.second()
-    tout.pass_on()
 
     def spatial_pair(pair, carry):
         spatial_records(pair).wait()
@@ -1212,14 +1257,15 @@
         refill(spatial_records, 8, pair)
         return carry
 
-    lax.fori_loop(0, PAIRS, spatial_pair, 0)
+    lax.fori_loop(0, PAIRS // 2, spatial_pair, 0)
+    fin.second(Z)
+    lax.fori_loop(PAIRS // 2, PAIRS, spatial_pair, 0)
     far = remote(work.far_send, work.far_recv, far_sems.at[0], far_sems.at[1], place.partner)
     far.start()
-    tqkv.pass_on()
-    fin.first_sent()
+    fin.relay_sent()
     sout.loaded()
     sout.first()
-    fout.third()
+    fin.second(XY)
     far.wait()
 
     def join(step, carry):
@@ -1233,14 +1279,18 @@
     project_back(sqkv_tiles, 14, 0, 2)
     sqkv.loaded()
     sqkv.first()
-    project_back(sqkv_tiles, 14, 2, 6)
+    fout.third()
+    project_back(sqkv_tiles, 14, 2, 4)
+    fin.direct_sent()
     sqkv.pass_on()
     sout.pass_on()
+    project_back(sqkv_tiles, 14, 4, 6)
     tout.second()
     tqkv.second()
+    fout.fourth()
+    fout.gather()
     kept1.wait()
     norm_back(total, 0, GAIN1, None, None)
-    fin.third()
 
     def finish_rows(step, carry):
         value = grad[pl.ds(pl.multiple_of(step * 32, 32), 32)]
@@ -1266,33 +1316,43 @@
         table = table + jnp.where(at_row == action, work.frame_sums[i : i + 1], 0.0)
     work.sums[0:8] = table
     small.begin()
-    fout.fourth()
+    fin.third()
+    small.step0()
+    sqkv.second()
     sout.second()
-    small.step0()
+    fout.spread()
     tout.third()
+    tqkv.third()
+    small.advance(0)
     fin.fourth()
-    sqkv.second()
-    small.advance(0)
-    tqkv.third()
+    fin.gather()
+    sqkv.third()
     sout.third()
     small.advance(1)
+    tout.fourth()
+    tout.gather()
+    tqkv.fourth()
+    tqkv.gather()
     fout.fifth()
-    sqkv.third()
-    tout.fourth()
+    fin.spread()
+    sqkv.fourth()
+    sqkv.gather()
+    sout.fourth()
+    sout.gather()
+    small.advance(2)
+    tout.spread()
+    tqkv.spread()
     fin.fifth()
-    small.advance(2)
-    tqkv.fourth()
-    sout.fourth()
-    sqkv.fourth()
+    sqkv.fifth()
+    sout.fifth()
     tout.fifth()
     tqkv.fifth()
-    sout.fifth()
-    sqkv.fifth()
     small.finish(outs.small_sums, io_sems.at[3])
     for one in reductions:
         one.finish()
     for one in (tout, tqkv, sout, sqkv):
-        one.first_sent()
+        one.relay_sent()
+        one.direct_sent()
     for one in (fout, fin, tout, sout, sqkv):
         one.rights_sent()
     back.sent()
@@ -1306,9 +1366,9 @@
     work = [pltpu.VMEM(shape, dtype) for shape, dtype in BACK_WORK.values()]
     work += [pltpu.VMEM((2, 4, 2, 4, k // 64, 2 * ROWS), BF16) for k, _, _ in MATRICES]
     work += [pltpu.VMEM((2 * ROWS, n // 2), BF16) for _, n, _ in MATRICES]
-    work += [pltpu.VMEM((k // 64, n // 2), BF16) for k, n, _ in MATRICES]
+    work += [pltpu.VMEM((2, k // 64, n // 2), BF16) for k, n, _ in MATRICES]
     work += [sem(shape) for shape in BACK_SEMS.values()]
-    shapes = list(BACK_OUTS.values()) + [((k // 8, n), BF16) for k, n, _ in MATRICES]
+    shapes = list(BACK_OUTS.values()) + [((2, 4, k // 64, n), BF16) for k, n, _ in MATRICES]
     in_keys, saved_keys, weight_keys = tuple(vars(ins)) + tuple(vars(scalars)), tuple(vars(saved)), tuple(vars(weights))
     return pl.pallas_call(
         functools.partial(backward_kernel, in_keys, saved_keys, weight_keys),
@@ -1358,11 +1418,12 @@
     plain_out = [refs.pop(0) for _ in range(passed)]
     table, vectors = refs.pop(0), [refs.pop(0) for _ in SUM_VECTORS]
     narrow_in, wide_out = refs[:count], refs[count : 2 * count]
-    sems = refs[2 * count]
+    between, sems = refs[2 * count : 2 * count + passed], refs[2 * count + passed]
     loads = [pltpu.make_async_copy(narrow[i], narrow_in[i], sems.at[0, i]) for i in range(count)]
     stores = [pltpu.make_async_copy(wide_out[i], wide[i], sems.at[1, i]) for i in range(count)]
-    moves = [pltpu.make_async_copy(plain[i], plain_out[i], sems.at[2, i]) for i in range(passed)]
-    for copy in loads + moves:
+    reads = [pltpu.make_async_copy(plain[i], between[i], sems.at[2, i]) for i in range(passed)]
+    moves = [pltpu.make_async_copy(between[i], plain_out[i], sems.at[3, i]) for i in range(passed)]
+    for copy in loads + reads:
         copy.start()
     table[...] = sums[0:8]
     for (row, rows), vector in zip(SUM_VECTORS, vectors):
@@ -1377,6 +1438,9 @@
 
         lax.fori_loop(0, narrow_in[i].shape[0] // 16, one, 0, unroll=2)
         stores[i].start()
+    for read, move in zip(reads, moves):
+        read.wait()
+        move.start()
     for copy in stores + moves:
         copy.wait()
 
@@ -1386,6 +1450,7 @@
     vectors = [jax.ShapeDtypeStruct((rows * WIDTH,), F32) for _, rows in SUM_VECTORS]
     shapes = [jax.ShapeDtypeStruct(one.shape, F32) for one in matrices]
     scratch = [pltpu.VMEM(one.shape, BF16) for one in matrices] + [pltpu.VMEM(one.shape, F32) for one in matrices]
+    scratch += [pltpu.VMEM(one.shape, one.dtype) for one in plain]
     results = pl.pallas_call(
         widen_kernel,
         out_shape=shapes
@@ -1394,7 +1459,7 @@
         + vectors,
         in_specs=[ANY] * (count + len(plain)) + [VMEM],
         out_specs=[ANY] * (count + len(plain)) + [VMEM] * (1 + len(vectors)),
-        scratch_shapes=scratch + [pltpu.SemaphoreType.DMA((3, count))],
+        scratch_shapes=scratch + [pltpu.SemaphoreType.DMA((4, count))],
         compiler_params=pltpu.CompilerParams(vmem_limit_bytes=62 * 2**20),
         cost_estimate=pl.CostEstimate(flops=0, bytes_accessed=14 * 2**20, transcendentals=0),
         name="widen",
@@ -1488,6 +1553,7 @@
         ),
         weights,
     )
+    matrices = [one.reshape(-1, one.shape[-1]) for one in matrices]
     matrices, passed, small = widen(matrices, (saved.big_out, saved.small_out, big_grad, small_grad), sums)
     g_fout, g_fin, g_tout, g_tqkv, g_sout, g_sqkv = matrices
     table, gain1, shift1, bias_s, gain2, shift2, bias_t, gain3, shift3, bias_in, bias_out = small

time: 261 us -> 210 us (0.80)
  Pallas kernels: 260 us -> 209 us
    pallas_call x1, Pallas kernels: 50.5 us -> 6.97 us  [widen(): pl.pallas_call(widen_kernel, out_shape=shapes + [jax.ShapeDtypeStruct(one...]
    pallas_call x1, Pallas kernels: 143 us -> 135 us  [backward(): pl.pallas_call(functools.partial(backward_kernel, in_keys, saved_keys, we...]
where the time goes in v3:
time: 210 us; the launch traced here: 209 us
  Pallas kernels  209 us (100%)
    pallas_call x1, Pallas kernels, backward(): pl.pallas_call(functools.partial(backward_kernel, in_keys, saved_keys, we...  135 us
    pallas_call x1, Pallas kernels, forward(): pl.pallas_call(functools.partial(forward_kernel, in_keys, len(vectors), w...  66.2 us
    pallas_call x1, Pallas kernels, widen(): pl.pallas_call(widen_kernel, out_shape=shapes + [jax.ShapeDtypeStruct(one...  6.97 us

profile of v3, /device:TPU:1, one launch (start us, length us, event | category | flops | bytes accessed | tf_op | source)
XLA Modules:
  0.0 209.5 jit_solution(1776194514215001949)
XLA Ops:
  0.7 66.2 %layer_forward.1 = (bf16[128,1024]{1,0:T(8,128)(2,1)}, bf16[128,1024]{1,0:T(8,128)(2,1)}, f32[256,1024]{1,0:T(8,128)}, f32[256,1024]{1,0:T(8,128)}, f32[256,1024...) custom-call(bf16[128,1024]{1,0:T(8,128)(2,1)} %bitcast.24, ...), custom_call_target="tpu_custom_call" | custom-call | flops 8999999488 | bytes 62914560 | tf_op jit(solution)/shard_map/layer_forward/pallas_call | solution.py:534
  66.9 135.4 %layer_backward.1 = (f32[128,1024]{1,0:T(8,128)}, f32[128,1024]{1,0:T(8,128)}, f32[24,1024]{1,0:T(8,128)}, bf16[2,4,64,1024]{3,2,1,0:T(8,128)(2,1)}, bf16[2,4,16...) custom-call(bf16[128,1024]{1,0:T(8,128)(2,1)} %bitcast.36, ...), custom_call_target="tpu_custom_call" | custom-call | flops 17999998976 | bytes 83886080 | tf_op jit(solution)/shard_map/layer_backward/pallas_call | solution.py:1373
  202.3 7.0 %widen.1 = (f32[512,1024]{1,0:T(8,128)}, f32[128,4096]{1,0:T(8,128)}, f32[128,1024]{1,0:T(8,128)}, f32[128,3072]{1,0:T(8,128)}, f32[128,1024]{1,0:T(8,128)}, /*i...) custom-call(bf16[512,1024]{1,0:T(8,128)(2,1)} %bitcast.20, ...), custom_call_target="tpu_custom_call" | custom-call | bytes 14680064 | tf_op jit(solution)/shard_map/widen/pallas_call | solution.py:1454
